TPU v7x, 256 devices: a whole 4x4x8 slice. The times are simulated.
256 devices in a mesh: dp: 8 (over z), section: 16 (over y_hi, x, core), mp: 2 (over y_lo).
Axes of the slice: x: 4, y: 4 (y_hi: 2, y_lo: 2; y = y_hi * 2 + y_lo), z: 8, core: 2. Of those that a mesh axis runs over, the one named last changes fastest.
Arguments:
- stash: bfloat16 [16, 4, 256, 6144], P('section', None, 'dp'), may hold values from -6 to 6
- w_mix: bfloat16 [16, 6144, 6144], P('section', 'dp', 'mp'), may hold values from -0.0390625 to 0.0390625
- top_grad: bfloat16 [4, 256, 6144], P(None, 'dp', 'mp'), may hold values from -6 to 6
- order: int32 [16, 4], P('section'), may hold values from 0 to 3, each once within a row
Outputs:
- input_grad: bfloat16 [16, 4, 256, 6144], P('section', None, 'dp', 'mp')
- grad_mix: bfloat16 [16, 6144, 6144], P('section', 'dp', 'mp')
Inputs may be any that keep to these rules, and one draw needn't show every extreme that they name: Each row of order names every micro-batch exactly once.
All inputs are finite; a program needn't handle non-finite values.
Results may differ from a plain program's by a relative error of at most 0.039.
Values may be sent and summed in bfloat16 or wider, within the bound.
A program may use at most 128 MiB of HBM per device.

v0:
```python
import jax
import jax.numpy as jnp
from jax import lax
from jax.sharding import PartitionSpec as P


def passed_along(shard, axis, by):
    size = lax.axis_size(axis)
    pairs = [(i, i + by) for i in range(size) if 0 <= i + by < size]
    return lax.ppermute(shard, axis, pairs)


def gelu_slope(value):
    inner = 0.7978845608 * (value + 0.044715 * value * value * value)
    tangent = jnp.tanh(inner)
    return 0.5 * (1.0 + tangent) + 0.5 * value * (1.0 - tangent * tangent) * 0.7978845608 * (
        1.0 + 3.0 * 0.044715 * value * value
    )


def chain_block(incoming, preactivation_value, block_weight, valid):
    hidden_grad = (incoming.astype(jnp.float32) * gelu_slope(preactivation_value)).astype(
        jnp.bfloat16
    )
    all_rows = lax.all_gather(hidden_grad, "dp", axis=0, tiled=True)

    def local_product():
        return lax.dot_general(
            all_rows, block_weight, (((1,), (1,)), ((), ())), preferred_element_type=jnp.float32
        ).astype(jnp.bfloat16)

    def empty_product():
        return jnp.zeros((all_rows.shape[0], block_weight.shape[0]), jnp.bfloat16)

    row_portion = lax.cond(valid, local_product, empty_product)
    returned = lax.all_to_all(row_portion, "dp", split_axis=0, concat_axis=1, tiled=True)
    summed = lax.psum_scatter(returned, "mp", scatter_dimension=1, tiled=True).astype(jnp.float32)
    return ((incoming.astype(jnp.float32) + summed).astype(jnp.bfloat16), all_rows)


def on_device(stash, w_mix, top_grad, order):
    section_count = lax.axis_size("section")
    section_place = lax.axis_index("section")
    dp_count = lax.axis_size("dp")
    micro = stash.shape[1]
    rows = stash.shape[2]
    weight_matrix = w_mix[0]
    half = weight_matrix.shape[1]
    series = jnp.arange(micro, dtype=jnp.int32)
    match = (order[0][None, :] == series[:, None]).astype(jnp.int32)
    slot_table = jnp.sum(series[None, :] * match, axis=1)
    x_own = jnp.take(stash[0], slot_table, axis=0)
    x_cols = lax.all_to_all(x_own, "dp", split_axis=2, concat_axis=1, tiled=True)
    pre_rows = lax.psum_scatter(
        jnp.einsum("mrd,df->rmf", x_cols, weight_matrix, preferred_element_type=jnp.float32).astype(
            jnp.bfloat16
        ),
        "dp",
        scatter_dimension=0,
        tiled=True,
    ).astype(jnp.float32)
    level = section_count - 1 - section_place
    total_steps = section_count - 1 + micro
    top_from = section_count - 1

    def advance(step, carry):
        received, out_buffer, hidden_buffer = carry
        which = step - level
        valid = jnp.logical_and(which >= 0, which < micro)
        clipped = jnp.clip(which, 0, micro - 1)
        from_top = lax.dynamic_index_in_dim(top_grad, clipped, 0, keepdims=False)
        incoming = jnp.where(section_place >= top_from, from_top, received)
        pre_now = lax.dynamic_index_in_dim(pre_rows, clipped, 1, keepdims=False)
        own_half, all_rows = chain_block(incoming, pre_now, weight_matrix, valid)
        kept_out = lax.dynamic_index_in_dim(out_buffer, clipped, 0, keepdims=False)
        out_buffer = lax.dynamic_update_index_in_dim(
            out_buffer, jnp.where(valid, own_half, kept_out), clipped, 0
        )
        kept_hidden = lax.dynamic_index_in_dim(hidden_buffer, clipped, 0, keepdims=False)
        hidden_buffer = lax.dynamic_update_index_in_dim(
            hidden_buffer, jnp.where(valid, all_rows, kept_hidden), clipped, 0
        )
        sent = passed_along(own_half, "section", -1)
        return (sent, out_buffer, hidden_buffer)

    start_carry = (
        jnp.zeros((rows, half), jnp.bfloat16),
        jnp.zeros((micro, rows, half), jnp.bfloat16),
        jnp.zeros((micro, rows * dp_count, half), jnp.bfloat16),
    )
    final = lax.fori_loop(0, total_steps, advance, start_carry)
    out_buffer = final[1]
    hidden_flat = final[2].reshape(micro * rows * dp_count, half)
    cols_flat = x_cols.reshape(micro * rows * dp_count, x_cols.shape[2])
    scale_factor = (micro * rows * dp_count) ** (-0.5)
    grad_block = scale_factor * lax.dot_general(
        cols_flat, hidden_flat, (((0,), (0,)), ((), ())), preferred_element_type=jnp.float32
    )
    return (out_buffer[None], grad_block.astype(jnp.bfloat16)[None])


def solution(mesh):
    in_specs = (
        P("section", None, "dp", None),
        P("section", "dp", "mp"),
        P(None, "dp", "mp"),
        P("section", None),
    )
    out_specs = (P("section", None, "dp", "mp"), P("section", "dp", "mp"))
    return jax.shard_map(
        on_device, mesh=mesh, in_specs=in_specs, out_specs=out_specs, check_vma=False
    )
```

profile of v0, /device:TPU:1, one launch (start us, length us, event | category | flops | bytes accessed | tf_op | source)
XLA Modules:
  0.0 1844.8 jit_solution(543683229277341339)
XLA Ops:
  27.7 47.4 %all_to_all.55 = bf16[8,2,49152]{2,1,0:T(2,128)(2,1)} all-to-all(bf16[8,2,49152]{2,1,0:T(2,128)(2,1)S(1)} %reshape.47), channel_id=1, replica_groups=mesh['dp'=8,'section'=16,'mp'=2] {'dp'}, dimensions={0} | all-to-all | bytes 3145728 | tf_op jit(solution)/shard_map/all_to_all | solution.py:53
  101.0 73.4 %reduce-scatter.3.cloned.1.call-done = bf16[32,4,3072]{2,0,1:T(8,128)(2,1)} async-done(((bf16[256,4,3072]{2,0,1:T(8,128)(2,1)}), bf16[32,4,3072]{2,0,1:T(8,128)(2,1)}) %reduce-scatter.3.cloned.1.call-update) | async-done | bytes 786448 | tf_op jit(solution)/shard_map/reduce_scatter | solution.py:54
  181.2 1647.7 %while.19 = (s32[]{:T(128)}, bf16[32,3072]{1,0:T(8,128)(2,1)S(1)}, bf16[4,32,3072]{2,1,0:T(8,128)(2,1)}, bf16[4,256,3072]{2,1,0:T(8,128)(2,1)}, pred[]{:T(512)},...) while((s32[]{:T(128)}, bf16[32,3072]{1,0:T(8,128)(2,1)S(1)}, ...), condition=%wide.region_6.7_spmd, body=%wide.region_2.6_spmd.sunk | while | flops 1211596800 | bytes 26542944 | solution.py:91
  183.3 35.3 %all-gather.2.cloned.1.call-done = bf16[256,3072]{1,0:T(8,128)(2,1)} async-done(((bf16[32,3072]{1,0:T(8,128)(2,1)}), bf16[256,3072]{1,0:T(8,128)(2,1)}) %all-gather.2.cloned.1.call-update) | async-done | bytes 1572880 | tf_op jit(solution)/shard_map/while/body/eval_jaxpr/all_gather | solution.py:25
  267.1 38.0 %all-gather.2.cloned.1.call-done = bf16[256,3072]{1,0:T(8,128)(2,1)} async-done(((bf16[32,3072]{1,0:T(8,128)(2,1)}), bf16[256,3072]{1,0:T(8,128)(2,1)}) %all-gather.2.cloned.1.call-update) | async-done | bytes 1572880 | tf_op jit(solution)/shard_map/while/body/eval_jaxpr/all_gather | solution.py:25
  322.8 21.5 %reduce-scatter.5.cloned.1.call-done = bf16[32,3072]{1,0:T(8,128)(2,1)} async-done(((bf16[32,6144]{1,0:T(8,128)(2,1)}), bf16[32,3072]{1,0:T(8,128)(2,1)}) %reduce-scatter.5.cloned.1.call-update) | async-done | bytes 196624 | tf_op jit(solution)/shard_map/while/body/eval_jaxpr/reduce_scatter | solution.py:37
  355.1 38.0 %all-gather.2.cloned.1.call-done = bf16[256,3072]{1,0:T(8,128)(2,1)} async-done(((bf16[32,3072]{1,0:T(8,128)(2,1)}), bf16[256,3072]{1,0:T(8,128)(2,1)}) %all-gather.2.cloned.1.call-update) | async-done | bytes 1572880 | tf_op jit(solution)/shard_map/while/body/eval_jaxpr/all_gather | solution.py:25
  410.7 21.5 %reduce-scatter.5.cloned.1.call-done = bf16[32,3072]{1,0:T(8,128)(2,1)} async-done(((bf16[32,6144]{1,0:T(8,128)(2,1)}), bf16[32,3072]{1,0:T(8,128)(2,1)}) %reduce-scatter.5.cloned.1.call-update) | async-done | bytes 196624 | tf_op jit(solution)/shard_map/while/body/eval_jaxpr/reduce_scatter | solution.py:37
  443.1 38.4 %all-gather.2.cloned.1.call-done = bf16[256,3072]{1,0:T(8,128)(2,1)} async-done(((bf16[32,3072]{1,0:T(8,128)(2,1)}), bf16[256,3072]{1,0:T(8,128)(2,1)}) %all-gather.2.cloned.1.call-update) | async-done | bytes 1572880 | tf_op jit(solution)/shard_map/while/body/eval_jaxpr/all_gather | solution.py:25
  499.1 21.8 %reduce-scatter.5.cloned.1.call-done = bf16[32,3072]{1,0:T(8,128)(2,1)} async-done(((bf16[32,6144]{1,0:T(8,128)(2,1)}), bf16[32,3072]{1,0:T(8,128)(2,1)}) %reduce-scatter.5.cloned.1.call-update) | async-done | bytes 196624 | tf_op jit(solution)/shard_map/while/body/eval_jaxpr/reduce_scatter | solution.py:37
  531.7 38.0 %all-gather.2.cloned.1.call-done = bf16[256,3072]{1,0:T(8,128)(2,1)} async-done(((bf16[32,3072]{1,0:T(8,128)(2,1)}), bf16[256,3072]{1,0:T(8,128)(2,1)}) %all-gather.2.cloned.1.call-update) | async-done | bytes 1572880 | tf_op jit(solution)/shard_map/while/body/eval_jaxpr/all_gather | solution.py:25
  587.4 21.8 %reduce-scatter.5.cloned.1.call-done = bf16[32,3072]{1,0:T(8,128)(2,1)} async-done(((bf16[32,6144]{1,0:T(8,128)(2,1)}), bf16[32,3072]{1,0:T(8,128)(2,1)}) %reduce-scatter.5.cloned.1.call-update) | async-done | bytes 196624 | tf_op jit(solution)/shard_map/while/body/eval_jaxpr/reduce_scatter | solution.py:37
  620.0 38.0 %all-gather.2.cloned.1.call-done = bf16[256,3072]{1,0:T(8,128)(2,1)} async-done(((bf16[32,3072]{1,0:T(8,128)(2,1)}), bf16[256,3072]{1,0:T(8,128)(2,1)}) %all-gather.2.cloned.1.call-update) | async-done | bytes 1572880 | tf_op jit(solution)/shard_map/while/body/eval_jaxpr/all_gather | solution.py:25
  675.7 21.8 %reduce-scatter.5.cloned.1.call-done = bf16[32,3072]{1,0:T(8,128)(2,1)} async-done(((bf16[32,6144]{1,0:T(8,128)(2,1)}), bf16[32,3072]{1,0:T(8,128)(2,1)}) %reduce-scatter.5.cloned.1.call-update) | async-done | bytes 196624 | tf_op jit(solution)/shard_map/while/body/eval_jaxpr/reduce_scatter | solution.py:37
  708.3 38.0 %all-gather.2.cloned.1.call-done = bf16[256,3072]{1,0:T(8,128)(2,1)} async-done(((bf16[32,3072]{1,0:T(8,128)(2,1)}), bf16[256,3072]{1,0:T(8,128)(2,1)}) %all-gather.2.cloned.1.call-update) | async-done | bytes 1572880 | tf_op jit(solution)/shard_map/while/body/eval_jaxpr/all_gather | solution.py:25
  764.0 21.8 %reduce-scatter.5.cloned.1.call-done = bf16[32,3072]{1,0:T(8,128)(2,1)} async-done(((bf16[32,6144]{1,0:T(8,128)(2,1)}), bf16[32,3072]{1,0:T(8,128)(2,1)}) %reduce-scatter.5.cloned.1.call-update) | async-done | bytes 196624 | tf_op jit(solution)/shard_map/while/body/eval_jaxpr/reduce_scatter | solution.py:37
  796.6 38.0 %all-gather.2.cloned.1.call-done = bf16[256,3072]{1,0:T(8,128)(2,1)} async-done(((bf16[32,3072]{1,0:T(8,128)(2,1)}), bf16[256,3072]{1,0:T(8,128)(2,1)}) %all-gather.2.cloned.1.call-update) | async-done | bytes 1572880 | tf_op jit(solution)/shard_map/while/body/eval_jaxpr/all_gather | solution.py:25
  852.3 20.2 %reduce-scatter.5.cloned.1.call-done = bf16[32,3072]{1,0:T(8,128)(2,1)} async-done(((bf16[32,6144]{1,0:T(8,128)(2,1)}), bf16[32,3072]{1,0:T(8,128)(2,1)}) %reduce-scatter.5.cloned.1.call-update) | async-done | bytes 196624 | tf_op jit(solution)/shard_map/while/body/eval_jaxpr/reduce_scatter | solution.py:37
  883.4 38.0 %all-gather.2.cloned.1.call-done = bf16[256,3072]{1,0:T(8,128)(2,1)} async-done(((bf16[32,3072]{1,0:T(8,128)(2,1)}), bf16[256,3072]{1,0:T(8,128)(2,1)}) %all-gather.2.cloned.1.call-update) | async-done | bytes 1572880 | tf_op jit(solution)/shard_map/while/body/eval_jaxpr/all_gather | solution.py:25
  939.1 20.2 %reduce-scatter.5.cloned.1.call-done = bf16[32,3072]{1,0:T(8,128)(2,1)} async-done(((bf16[32,6144]{1,0:T(8,128)(2,1)}), bf16[32,3072]{1,0:T(8,128)(2,1)}) %reduce-scatter.5.cloned.1.call-update) | async-done | bytes 196624 | tf_op jit(solution)/shard_map/while/body/eval_jaxpr/reduce_scatter | solution.py:37
  970.2 38.1 %all-gather.2.cloned.1.call-done = bf16[256,3072]{1,0:T(8,128)(2,1)} async-done(((bf16[32,3072]{1,0:T(8,128)(2,1)}), bf16[256,3072]{1,0:T(8,128)(2,1)}) %all-gather.2.cloned.1.call-update) | async-done | bytes 1572880 | tf_op jit(solution)/shard_map/while/body/eval_jaxpr/all_gather | solution.py:25
  1056.7 38.4 %all-gather.2.cloned.1.call-done = bf16[256,3072]{1,0:T(8,128)(2,1)} async-done(((bf16[32,3072]{1,0:T(8,128)(2,1)}), bf16[256,3072]{1,0:T(8,128)(2,1)}) %all-gather.2.cloned.1.call-update) | async-done | bytes 1572880 | tf_op jit(solution)/shard_map/while/body/eval_jaxpr/all_gather | solution.py:25
  1143.5 38.1 %all-gather.2.cloned.1.call-done = bf16[256,3072]{1,0:T(8,128)(2,1)} async-done(((bf16[32,3072]{1,0:T(8,128)(2,1)}), bf16[256,3072]{1,0:T(8,128)(2,1)}) %all-gather.2.cloned.1.call-update) | async-done | bytes 1572880 | tf_op jit(solution)/shard_map/while/body/eval_jaxpr/all_gather | solution.py:25
  1199.2 20.2 %reduce-scatter.5.cloned.1.call-done = bf16[32,3072]{1,0:T(8,128)(2,1)} async-done(((bf16[32,6144]{1,0:T(8,128)(2,1)}), bf16[32,3072]{1,0:T(8,128)(2,1)}) %reduce-scatter.5.cloned.1.call-update) | async-done | bytes 196624 | tf_op jit(solution)/shard_map/while/body/eval_jaxpr/reduce_scatter | solution.py:37
  1230.3 38.0 %all-gather.2.cloned.1.call-done = bf16[256,3072]{1,0:T(8,128)(2,1)} async-done(((bf16[32,3072]{1,0:T(8,128)(2,1)}), bf16[256,3072]{1,0:T(8,128)(2,1)}) %all-gather.2.cloned.1.call-update) | async-done | bytes 1572880 | tf_op jit(solution)/shard_map/while/body/eval_jaxpr/all_gather | solution.py:25
  1317.0 38.3 %all-gather.2.cloned.1.call-done = bf16[256,3072]{1,0:T(8,128)(2,1)} async-done(((bf16[32,3072]{1,0:T(8,128)(2,1)}), bf16[256,3072]{1,0:T(8,128)(2,1)}) %all-gather.2.cloned.1.call-update) | async-done | bytes 1572880 | tf_op jit(solution)/shard_map/while/body/eval_jaxpr/all_gather | solution.py:25
  1373.0 20.2 %reduce-scatter.5.cloned.1.call-done = bf16[32,3072]{1,0:T(8,128)(2,1)} async-done(((bf16[32,6144]{1,0:T(8,128)(2,1)}), bf16[32,3072]{1,0:T(8,128)(2,1)}) %reduce-scatter.5.cloned.1.call-update) | async-done | bytes 196624 | tf_op jit(solution)/shard_map/while/body/eval_jaxpr/reduce_scatter | solution.py:37
  1404.1 38.0 %all-gather.2.cloned.1.call-done = bf16[256,3072]{1,0:T(8,128)(2,1)} async-done(((bf16[32,3072]{1,0:T(8,128)(2,1)}), bf16[256,3072]{1,0:T(8,128)(2,1)}) %all-gather.2.cloned.1.call-update) | async-done | bytes 1572880 | tf_op jit(solution)/shard_map/while/body/eval_jaxpr/all_gather | solution.py:25
  1490.9 38.3 %all-gather.2.cloned.1.call-done = bf16[256,3072]{1,0:T(8,128)(2,1)} async-done(((bf16[32,3072]{1,0:T(8,128)(2,1)}), bf16[256,3072]{1,0:T(8,128)(2,1)}) %all-gather.2.cloned.1.call-update) | async-done | bytes 1572880 | tf_op jit(solution)/shard_map/while/body/eval_jaxpr/all_gather | solution.py:25
  1576.4 38.3 %all-gather.2.cloned.1.call-done = bf16[256,3072]{1,0:T(8,128)(2,1)} async-done(((bf16[32,3072]{1,0:T(8,128)(2,1)}), bf16[256,3072]{1,0:T(8,128)(2,1)}) %all-gather.2.cloned.1.call-update) | async-done | bytes 1572880 | tf_op jit(solution)/shard_map/while/body/eval_jaxpr/all_gather | solution.py:25
  1662.0 38.0 %all-gather.2.cloned.1.call-done = bf16[256,3072]{1,0:T(8,128)(2,1)} async-done(((bf16[32,3072]{1,0:T(8,128)(2,1)}), bf16[256,3072]{1,0:T(8,128)(2,1)}) %all-gather.2.cloned.1.call-update) | async-done | bytes 1572880 | tf_op jit(solution)/shard_map/while/body/eval_jaxpr/all_gather | solution.py:25
  1746.4 38.4 %all-gather.2.cloned.1.call-done = bf16[256,3072]{1,0:T(8,128)(2,1)} async-done(((bf16[32,3072]{1,0:T(8,128)(2,1)}), bf16[256,3072]{1,0:T(8,128)(2,1)}) %all-gather.2.cloned.1.call-update) | async-done | bytes 1572880 | tf_op jit(solution)/shard_map/while/body/eval_jaxpr/all_gather | solution.py:25
  (316 shorter events, 793.5 us)
Async XLA Ops:
  7.2 167.2 %reduce-scatter.3.cloned.1.call-start = ((), (), s32[]{:S(2)}) async-start(), calls=%async_computation.4 | async-start | bytes 7077888 | tf_op jit(solution)/shard_map/reduce_scatter | solution.py:54
  183.3 72.9 %reduce-scatter.5.cloned.1.call-start = ((), (), s32[]{:S(2)}) async-start(), calls=%async_computation.6 | async-start | bytes 589824 | tf_op jit(solution)/shard_map/while/body/eval_jaxpr/reduce_scatter | solution.py:37
  265.0 40.1 %all-gather.2.cloned.1.call-start = ((), (), s32[]{:S(2)}) async-start(), calls=%async_computation.5 | async-start | bytes 1769472 | tf_op jit(solution)/shard_map/while/body/eval_jaxpr/all_gather | solution.py:25
  267.0 77.2 %reduce-scatter.5.cloned.1.call-start = ((), (), s32[]{:S(2)}) async-start(), calls=%async_computation.6 | async-start | bytes 589824 | tf_op jit(solution)/shard_map/while/body/eval_jaxpr/reduce_scatter | solution.py:37
  355.0 77.2 %reduce-scatter.5.cloned.1.call-start = ((), (), s32[]{:S(2)}) async-start(), calls=%async_computation.6 | async-start | bytes 589824 | tf_op jit(solution)/shard_map/while/body/eval_jaxpr/reduce_scatter | solution.py:37
  441.0 40.4 %all-gather.2.cloned.1.call-start = ((), (), s32[]{:S(2)}) async-start(), calls=%async_computation.5 | async-start | bytes 1769472 | tf_op jit(solution)/shard_map/while/body/eval_jaxpr/all_gather | solution.py:25
  443.0 77.8 %reduce-scatter.5.cloned.1.call-start = ((), (), s32[]{:S(2)}) async-start(), calls=%async_computation.6 | async-start | bytes 589824 | tf_op jit(solution)/shard_map/while/body/eval_jaxpr/reduce_scatter | solution.py:37
  529.6 40.1 %all-gather.2.cloned.1.call-start = ((), (), s32[]{:S(2)}) async-start(), calls=%async_computation.5 | async-start | bytes 1769472 | tf_op jit(solution)/shard_map/while/body/eval_jaxpr/all_gather | solution.py:25
  531.7 77.5 %reduce-scatter.5.cloned.1.call-start = ((), (), s32[]{:S(2)}) async-start(), calls=%async_computation.6 | async-start | bytes 589824 | tf_op jit(solution)/shard_map/while/body/eval_jaxpr/reduce_scatter | solution.py:37
  620.0 77.5 %reduce-scatter.5.cloned.1.call-start = ((), (), s32[]{:S(2)}) async-start(), calls=%async_computation.6 | async-start | bytes 589824 | tf_op jit(solution)/shard_map/while/body/eval_jaxpr/reduce_scatter | solution.py:37
  708.3 77.5 %reduce-scatter.5.cloned.1.call-start = ((), (), s32[]{:S(2)}) async-start(), calls=%async_computation.6 | async-start | bytes 589824 | tf_op jit(solution)/shard_map/while/body/eval_jaxpr/reduce_scatter | solution.py:37
  794.5 40.1 %all-gather.2.cloned.1.call-start = ((), (), s32[]{:S(2)}) async-start(), calls=%async_computation.5 | async-start | bytes 1769472 | tf_op jit(solution)/shard_map/while/body/eval_jaxpr/all_gather | solution.py:25
  796.6 76.0 %reduce-scatter.5.cloned.1.call-start = ((), (), s32[]{:S(2)}) async-start(), calls=%async_computation.6 | async-start | bytes 589824 | tf_op jit(solution)/shard_map/while/body/eval_jaxpr/reduce_scatter | solution.py:37
  881.3 40.1 %all-gather.2.cloned.1.call-start = ((), (), s32[]{:S(2)}) async-start(), calls=%async_computation.5 | async-start | bytes 1769472 | tf_op jit(solution)/shard_map/while/body/eval_jaxpr/all_gather | solution.py:25
  883.3 76.0 %reduce-scatter.5.cloned.1.call-start = ((), (), s32[]{:S(2)}) async-start(), calls=%async_computation.6 | async-start | bytes 589824 | tf_op jit(solution)/shard_map/while/body/eval_jaxpr/reduce_scatter | solution.py:37
  968.1 40.1 %all-gather.2.cloned.1.call-start = ((), (), s32[]{:S(2)}) async-start(), calls=%async_computation.5 | async-start | bytes 1769472 | tf_op jit(solution)/shard_map/while/body/eval_jaxpr/all_gather | solution.py:25
  970.1 75.7 %reduce-scatter.5.cloned.1.call-start = ((), (), s32[]{:S(2)}) async-start(), calls=%async_computation.6 | async-start | bytes 589824 | tf_op jit(solution)/shard_map/while/body/eval_jaxpr/reduce_scatter | solution.py:37
  1054.6 40.5 %all-gather.2.cloned.1.call-start = ((), (), s32[]{:S(2)}) async-start(), calls=%async_computation.5 | async-start | bytes 1769472 | tf_op jit(solution)/shard_map/while/body/eval_jaxpr/all_gather | solution.py:25
  1056.6 76.0 %reduce-scatter.5.cloned.1.call-start = ((), (), s32[]{:S(2)}) async-start(), calls=%async_computation.6 | async-start | bytes 589824 | tf_op jit(solution)/shard_map/while/body/eval_jaxpr/reduce_scatter | solution.py:37
  1141.4 40.1 %all-gather.2.cloned.1.call-start = ((), (), s32[]{:S(2)}) async-start(), calls=%async_computation.5 | async-start | bytes 1769472 | tf_op jit(solution)/shard_map/while/body/eval_jaxpr/all_gather | solution.py:25
  1143.4 76.0 %reduce-scatter.5.cloned.1.call-start = ((), (), s32[]{:S(2)}) async-start(), calls=%async_computation.6 | async-start | bytes 589824 | tf_op jit(solution)/shard_map/while/body/eval_jaxpr/reduce_scatter | solution.py:37
  1230.2 75.9 %reduce-scatter.5.cloned.1.call-start = ((), (), s32[]{:S(2)}) async-start(), calls=%async_computation.6 | async-start | bytes 589824 | tf_op jit(solution)/shard_map/while/body/eval_jaxpr/reduce_scatter | solution.py:37
  1315.0 40.4 %all-gather.2.cloned.1.call-start = ((), (), s32[]{:S(2)}) async-start(), calls=%async_computation.5 | async-start | bytes 1769472 | tf_op jit(solution)/shard_map/while/body/eval_jaxpr/all_gather | solution.py:25
  1317.0 76.3 %reduce-scatter.5.cloned.1.call-start = ((), (), s32[]{:S(2)}) async-start(), calls=%async_computation.6 | async-start | bytes 589824 | tf_op jit(solution)/shard_map/while/body/eval_jaxpr/reduce_scatter | solution.py:37
  1404.1 76.0 %reduce-scatter.5.cloned.1.call-start = ((), (), s32[]{:S(2)}) async-start(), calls=%async_computation.6 | async-start | bytes 589824 | tf_op jit(solution)/shard_map/while/body/eval_jaxpr/reduce_scatter | solution.py:37
  1488.8 40.4 %all-gather.2.cloned.1.call-start = ((), (), s32[]{:S(2)}) async-start(), calls=%async_computation.5 | async-start | bytes 1769472 | tf_op jit(solution)/shard_map/while/body/eval_jaxpr/all_gather | solution.py:25
  1490.8 74.7 %reduce-scatter.5.cloned.1.call-start = ((), (), s32[]{:S(2)}) async-start(), calls=%async_computation.6 | async-start | bytes 589824 | tf_op jit(solution)/shard_map/while/body/eval_jaxpr/reduce_scatter | solution.py:37
  1574.4 40.4 %all-gather.2.cloned.1.call-start = ((), (), s32[]{:S(2)}) async-start(), calls=%async_computation.5 | async-start | bytes 1769472 | tf_op jit(solution)/shard_map/while/body/eval_jaxpr/all_gather | solution.py:25
  1576.4 74.7 %reduce-scatter.5.cloned.1.call-start = ((), (), s32[]{:S(2)}) async-start(), calls=%async_computation.6 | async-start | bytes 589824 | tf_op jit(solution)/shard_map/while/body/eval_jaxpr/reduce_scatter | solution.py:37
  1661.9 73.5 %reduce-scatter.5.cloned.1.call-start = ((), (), s32[]{:S(2)}) async-start(), calls=%async_computation.6 | async-start | bytes 589824 | tf_op jit(solution)/shard_map/while/body/eval_jaxpr/reduce_scatter | solution.py:37
  1744.3 40.4 %all-gather.2.cloned.1.call-start = ((), (), s32[]{:S(2)}) async-start(), calls=%async_computation.5 | async-start | bytes 1769472 | tf_op jit(solution)/shard_map/while/body/eval_jaxpr/all_gather | solution.py:25
  1746.3 73.8 %reduce-scatter.5.cloned.1.call-start = ((), (), s32[]{:S(2)}) async-start(), calls=%async_computation.6 | async-start | bytes 589824 | tf_op jit(solution)/shard_map/while/body/eval_jaxpr/reduce_scatter | solution.py:37
  (28 other events, 422.0 us)
Sparse Core Ops, SparseCore 0:
  101.1 73.2 reduce-scatter.2
  183.9 34.7 all-gather.1
  233.9 22.2 reduce-scatter.4
  267.3 37.7 all-gather.1
  320.4 23.7 reduce-scatter.4
  355.3 37.7 all-gather.1
  408.4 23.7 reduce-scatter.4
  443.6 37.7 all-gather.1
  496.7 24.0 reduce-scatter.4
  531.9 37.7 all-gather.1
  585.0 24.0 reduce-scatter.4
  620.2 37.7 all-gather.1
  673.3 24.0 reduce-scatter.4
  708.5 37.7 all-gather.1
  761.6 24.0 reduce-scatter.4
  796.8 37.7 all-gather.1
  849.9 22.5 reduce-scatter.4
  883.6 37.7 all-gather.1
  936.7 22.5 reduce-scatter.4
  970.4 37.7 all-gather.1
  1057.2 37.7 all-gather.1
  1143.7 37.7 all-gather.1
  1196.8 22.5 reduce-scatter.4
  1230.5 37.7 all-gather.1
  1283.6 22.5 reduce-scatter.4
  1317.6 37.7 all-gather.1
  1370.7 22.5 reduce-scatter.4
  1404.3 37.7 all-gather.1
  1491.4 37.7 all-gather.1
  1577.0 37.7 all-gather.1
  1662.2 37.7 all-gather.1
  1746.9 37.7 all-gather.1
  (7 shorter events, 129.8 us)
where the time goes:
time: 1850 us; the launch traced here: 1840 us
  waiting for transfers between devices  1210 us (65%)
  blocking collectives  322 us (17%)
  other arithmetic  116 us (6%)
  local copies, waits for them, and re-layouts  101 us (5%)
  starting transfers between devices  49.6 us (3%)
  matrix products  35.8 us (2%)
    all_gather x19, waiting for transfers between devices, chain_block(): all_rows = lax.all_gather(hidden_grad, 'dp', axis=0, tiled=True)  722 us
    reduce_scatter x19, waiting for transfers between devices, chain_block(): lax.psum_scatter(returned, 'mp', scatter_dimension=1, tiled=True)  365 us
    all_to_all x19, blocking collectives, chain_block(): lax.all_to_all(row_portion, 'dp', split_axis=0, concat_axis=1, tiled=True)  274 us
    reduce_scatter x1, waiting for transfers between devices, on_device(): lax.psum_scatter(jnp.einsum('mrd,df->rmf', x_cols, weight_matrix, preferr...  73.4 us
    ppermute x19, starting transfers between devices, passed_along(): return lax.ppermute(shard, axis, pairs)  48.8 us
    all_to_all x1, blocking collectives, on_device(): lax.all_to_all(x_own, 'dp', split_axis=2, concat_axis=1, tiled=True)  47.4 us
    ppermute x19, waiting for transfers between devices, passed_along(): return lax.ppermute(shard, axis, pairs)  44.8 us
    dynamic_update_slice x19, other arithmetic, advance(): lax.dynamic_update_index_in_dim(hidden_buffer, jnp.where(valid, all_rows,...  39 us
  transfers between devices with their start and end apart: 58, of which 58 were waited for; matrix products, arithmetic and copies ran while one was open for 5% of the time, Pallas kernels for 0%

commit v1 on v0

v1 whole, which is shorter than its diff:
```python
import jax
import jax.numpy as jnp
from jax import lax
from jax.experimental import pallas as pl
from jax.experimental.pallas import tpu as pltpu
from jax.sharding import PartitionSpec as P

MESH = pl.DeviceIdType.MESH


def gelu_slope(value):
    inner = 0.7978845608 * (value + 0.044715 * value * value * value)
    tangent = jnp.tanh(inner)
    return 0.5 * (1.0 + tangent) + 0.5 * value * (1.0 - tangent * tangent) * 0.7978845608 * (
        1.0 + 3.0 * 0.044715 * value * value
    )


def relay_kernel(w, slope, top, hidden_out, grad_out, h, inbox, carried, product, in_sem, h_sem, out_sem, copy_sem, flush_sem):
    nz, ns = lax.axis_size("dp"), lax.axis_size("section")
    z, s, m = lax.axis_index("dp"), lax.axis_index("section"), lax.axis_index("mp")
    chunks, rows, columns = h.shape
    block = columns // nz
    quarter = nz // 4
    above, below = lax.rem(s + 1, ns), lax.rem(s + ns - 1, ns)
    is_top = s == ns - 1
    owned = lax.rem(z + nz + quarter * (1 - 2 * m), nz)
    source = m * (nz // 2) + owned // 2
    to_m = z // (nz // 2)
    first = 2 * lax.rem(z, nz // 2) + nz - quarter * (1 - 2 * to_m)
    owners = [lax.rem(first, nz), lax.rem(first + 1, nz)]
    mine = pl.ds(pl.multiple_of(owned * block, block), block)

    barrier = pltpu.get_barrier_semaphore()
    for step in range(1, nz):
        pl.semaphore_signal(barrier, inc=1, device_id=(lax.rem(z + step, nz), s, m), device_id_type=MESH)
    pl.semaphore_signal(barrier, inc=1, device_id=(z, above, m), device_id_type=MESH)
    for part in range(2):
        pl.semaphore_signal(barrier, inc=1, device_id=(source, above, part), device_id_type=MESH)
    pl.semaphore_wait(barrier, nz + 2)

    def received(c):
        pltpu.make_async_copy(inbox.at[c], inbox.at[c], in_sem.at[c]).wait()
        unit_sum = inbox[c, 0].astype(jnp.float32) + inbox[c, 1].astype(jnp.float32)
        return (inbox[c, 2].astype(jnp.float32) + unit_sum).astype(jnp.bfloat16)

    def advance(c, _):
        @pl.when(is_top)
        def _():
            carried[c] = top[c]

        @pl.when(jnp.logical_not(is_top))
        def _():
            value = received(c)
            carried[c] = value
            grad_out[c] = value

        pltpu.make_async_remote_copy(
            src_ref=carried.at[c],
            dst_ref=inbox.at[c, 2],
            send_sem=out_sem.at[c],
            recv_sem=in_sem.at[c],
            device_id=(z, below, m),
            device_id_type=MESH,
        ).start()
        h[c, :, mine] = (carried[c].astype(jnp.float32) * slope[c]).astype(jnp.bfloat16)
        for step in range(1, nz):
            pltpu.make_async_remote_copy(
                src_ref=h.at[c, :, mine],
                dst_ref=h.at[c, :, mine],
                send_sem=copy_sem.at[c],
                recv_sem=h_sem.at[c],
                device_id=(lax.rem(z + step, nz), s, m),
                device_id_type=MESH,
            ).start()
        others = h.at[c, :, pl.ds(0, (nz - 1) * block)]
        pltpu.make_async_copy(others, others, h_sem.at[c]).wait()
        pltpu.make_async_copy(h.at[c], hidden_out.at[c], flush_sem.at[c]).start()
        value = lax.dot_general(
            h[c], w[...], (((1,), (1,)), ((), ())), preferred_element_type=jnp.float32
        ).astype(jnp.bfloat16)
        for part in range(2):
            product[c, part] = value[:, part * block : (part + 1) * block]
            pltpu.make_async_remote_copy(
                src_ref=product.at[c, part],
                dst_ref=inbox.at[c, m],
                send_sem=out_sem.at[c],
                recv_sem=in_sem.at[c],
                device_id=(owners[part], below, to_m),
                device_id_type=MESH,
            ).start()
        return 0

    lax.fori_loop(0, chunks, advance, 0)

    @pl.when(is_top)
    def _():
        def last(c, _):
            grad_out[c] = received(c)
            return 0

        lax.fori_loop(0, chunks, last, 0)

    def drain(c, _):
        others = h.at[c, :, pl.ds(0, (nz - 1) * block)]
        pltpu.make_async_copy(others, others, copy_sem.at[c]).wait()
        pltpu.make_async_copy(inbox.at[c], inbox.at[c], out_sem.at[c]).wait()
        pltpu.make_async_copy(h.at[c], hidden_out.at[c], flush_sem.at[c]).wait()
        return 0

    lax.fori_loop(0, chunks, drain, 0)


def relay(w, slope, top, chunks):
    depth, columns = w.shape
    tokens, block = slope.shape
    rows = tokens // chunks
    hidden, grad = pl.pallas_call(
        relay_kernel,
        out_shape=(
            jax.ShapeDtypeStruct((chunks, rows, columns), jnp.bfloat16),
            jax.ShapeDtypeStruct((chunks, rows, block), jnp.bfloat16),
        ),
        in_specs=[pl.BlockSpec(memory_space=pltpu.VMEM)] * 3,
        out_specs=(pl.BlockSpec(memory_space=pl.ANY), pl.BlockSpec(memory_space=pltpu.VMEM)),
        scratch_shapes=[
            pltpu.VMEM((chunks, rows, columns), jnp.bfloat16),
            pltpu.VMEM((chunks, 3, rows, block), jnp.bfloat16),
            pltpu.VMEM((chunks, rows, block), jnp.bfloat16),
            pltpu.VMEM((chunks, 2, rows, block), jnp.bfloat16),
            pltpu.SemaphoreType.DMA((chunks,)),
            pltpu.SemaphoreType.DMA((chunks,)),
            pltpu.SemaphoreType.DMA((chunks,)),
            pltpu.SemaphoreType.DMA((chunks,)),
            pltpu.SemaphoreType.DMA((chunks,)),
        ],
        compiler_params=pltpu.CompilerParams(
            collective_id=0, has_side_effects=True, vmem_limit_bytes=40 * 1024 * 1024
        ),
        cost_estimate=pl.CostEstimate(
            flops=2 * tokens * depth * columns,
            bytes_accessed=2 * (depth + tokens) * columns,
            transcendentals=0,
        ),
    )(w, slope.reshape(chunks, rows, block), top.reshape(chunks, rows, block))
    return hidden.reshape(tokens, columns), grad.reshape(tokens, block)


def on_device(stash, w_mix, top_grad, order):
    nz, ns = lax.axis_size("dp"), lax.axis_size("section")
    m = lax.axis_index("mp")
    micro, rows = stash.shape[1], stash.shape[2]
    tokens = micro * rows * nz
    weight = w_mix[0]
    depth, half = weight.shape
    block = half // nz
    turn = (nz // 4) * (1 - 2 * m)

    series = jnp.arange(micro, dtype=jnp.int32)
    match = (order[0][None, :] == series[:, None]).astype(jnp.int32)
    slot_table = jnp.sum(series[None, :] * match, axis=1)
    x_own = jnp.take(stash[0], slot_table, axis=0)
    x_cols = lax.all_to_all(x_own, "dp", split_axis=2, concat_axis=1, tiled=True)
    x_flat = x_cols.reshape(tokens, depth)

    turned = jnp.roll(weight.reshape(depth, nz, block), -turn, axis=1)
    partial = jnp.einsum("td,dzb->ztb", x_flat, turned, preferred_element_type=jnp.float32)
    pre = lax.psum_scatter(partial.astype(jnp.bfloat16), "dp", scatter_dimension=0, tiled=False)
    slope = gelu_slope(pre.astype(jnp.float32))

    top_blocks = jnp.roll(top_grad.reshape(micro, rows, nz, block), -turn, axis=2)
    top = lax.all_to_all(top_blocks, "dp", split_axis=2, concat_axis=1, tiled=True).reshape(tokens, block)

    hidden, grad = relay(weight, slope, top, tokens // rows)

    grad = lax.ppermute(grad, "section", [(i, (i + 1) % ns) for i in range(ns)])
    back = lax.all_to_all(grad.reshape(micro, nz, rows, block), "dp", split_axis=1, concat_axis=1, tiled=True)
    back = jnp.roll(back, turn, axis=1)
    input_grad = jnp.transpose(back, (0, 2, 1, 3)).reshape(micro, rows, half)

    grad_mix = tokens ** (-0.5) * lax.dot_general(
        x_flat, hidden, (((0,), (0,)), ((), ())), preferred_element_type=jnp.float32
    )
    return (input_grad[None], grad_mix.astype(jnp.bfloat16)[None])


def solution(mesh):
    in_specs = (
        P("section", None, "dp", None),
        P("section", "dp", "mp"),
        P(None, "dp", "mp"),
        P("section", None),
    )
    out_specs = (P("section", None, "dp", "mp"), P("section", "dp", "mp"))
    return jax.shard_map(
        on_device, mesh=mesh, in_specs=in_specs, out_specs=out_specs, check_vma=False
    )
```

time: 1850 us -> 742 us (0.40)
  waiting for transfers between devices: 1210 us -> 113 us
  Pallas kernels: 0 us -> 482 us
  blocking collectives: 322 us -> 29.9 us
  other arithmetic: 116 us -> 5.48 us
  local copies, waits for them, and re-layouts: 101 us -> 51 us
  starting transfers between devices: 49.6 us -> 12.8 us
    all_gather x19 -> x0, waiting for transfers between devices: 722 us -> none  [chain_block(): all_rows = lax.all_gather(hidden_grad, 'dp', axis=0, tiled=True)]
    pallas_call x0 -> x1, Pallas kernels: none -> 482 us  [relay(): pl.pallas_call(relay_kernel, out_shape=(jax.ShapeDtypeStruct((chunks, row...]
    reduce_scatter x20 -> x1, waiting for transfers between devices: 439 us -> 54.5 us  [on_device(): lax.psum_scatter(partial.astype(jnp.bfloat16), 'dp', scatter_dimension=0,...]
    all_to_all x20 -> x1, blocking collectives: 322 us -> 29.9 us  [on_device(): lax.all_to_all(top_blocks, 'dp', split_axis=2, concat_axis=1, tiled=True)]
    dynamic_update_slice x38 -> x0, other arithmetic: 73.2 us -> none  [the longest x19 39 us: advance(): lax.dynamic_update_index_in_dim(hidden_buffer, jnp.where(valid, all_rows,...]
    ppermute x19 -> x1, starting transfers between devices: 48.8 us -> 0.01 us  [on_device(): grad = lax.ppermute(grad, 'section', [(i, (i + 1) % ns) for i in range(ns)])]
    dynamic_slice x38 -> x1, local copies, waits for them, and re-layouts: 46.8 us -> 0.11 us  [on_device(): jnp.roll(top_grad.reshape(micro, rows, nz, block), -turn, axis=2)]
    convert_element_type x20 -> x0, other arithmetic: 40.4 us -> none  [the longest x19 38 us: chain_block(): (incoming.astype(jnp.float32) * gelu_slope(preactivation_value)).astype(j...]
  transfers between devices with their start and end apart: 58 -> 4, of which waited for: 58 -> 4; matrix products, arithmetic and copies ran while one was open for 5% -> 2% of each run, Pallas kernels for 0% -> 0%
where the time goes in v1:
time: 742 us; the launch traced here: 728 us
  Pallas kernels  482 us (65%)
  waiting for transfers between devices  113 us (15%)
  local copies, waits for them, and re-layouts  51 us (7%)
  blocking collectives  29.9 us (4%)
  matrix products  19.2 us (3%)
  between operations  14.2 us (2%)
  starting transfers between devices  12.8 us (2%)
    pallas_call x1, Pallas kernels, relay(): pl.pallas_call(relay_kernel, out_shape=(jax.ShapeDtypeStruct((chunks, row...  482 us
    reduce_scatter x1, waiting for transfers between devices, on_device(): lax.psum_scatter(partial.astype(jnp.bfloat16), 'dp', scatter_dimension=0,...  54.5 us
    all_to_all x1, waiting for transfers between devices, on_device(): lax.all_to_all(x_own, 'dp', split_axis=2, concat_axis=1, tiled=True)  31.6 us
    all_to_all x1, blocking collectives, on_device(): lax.all_to_all(top_blocks, 'dp', split_axis=2, concat_axis=1, tiled=True)  29.9 us
    unnamed x14, local copies, waits for them, and re-layouts  28.3 us
    ppermute x1, waiting for transfers between devices, on_device(): grad = lax.ppermute(grad, 'section', [(i, (i + 1) % ns) for i in range(ns)])  21 us
  transfers between devices with their start and end apart: 4, of which 4 were waited for; matrix products, arithmetic and copies ran while one was open for 2% of the time, Pallas kernels for 0%

profile of v1, /device:TPU:1, one launch (start us, length us, event | category | flops | bytes accessed | tf_op | source)
XLA Modules:
  0.0 728.0 jit_solution(16672483214184137100)
XLA Ops:
  7.2 0.9 select_reduce_fusion
  8.1 0.5 copy-done
  8.6 0.6 gather_fusion
  9.2 1.4 broadcast_select_fusion
  10.6 8.5 %copy.25 = bf16[4,32,6144]{1,0,2:T(4,128)(2,1)} copy(bf16[4,32,6144]{2,1,0:T(8,128)(2,1)} %broadcast_select_fusion) | data formatting | bytes 3145728 | tf_op jit(solution)/shard_map/jit(_take)/select_n | solution.py:162
  19.1 9.5 %reshape.58 = bf16[8,2,49152]{2,1,0:T(2,128)(2,1)} reshape(bf16[6144,4,32]{2,1,0:T(4,128)(2,1)} %bitcast.44) | data formatting | bytes 3145728
  28.6 9.0 %all-to-all-start = ((bf16[8,2,49152]{2,1,0:T(2,128)(2,1)}), bf16[8,2,49152]{2,1,0:T(2,128)(2,1)S(1)}, u32[]{:S(2)}, u32[]{:S(2)}) async-start(bf16[8,2,49152]{2,1,0:T(2,128)(2,1)} %reshape.58), calls=%async_computation | async-start | bytes 3145728 | tf_op jit(solution)/shard_map/all_to_all | solution.py:163
  37.7 6.6 copy.24
  44.3 31.6 %all-to-all-done = bf16[8,2,49152]{2,1,0:T(2,128)(2,1)S(1)} async-done(((bf16[8,2,49152]{2,1,0:T(2,128)(2,1)}), bf16[8,2,49152]{2,1,0:T(2,128)(2,1)S(1)}, u32[]{:S(2)}, u32[]{:S(2)}) %all-to-all-start) | async-done | bytes 1572896 | tf_op jit(solution)/shard_map/all_to_all | solution.py:163
  75.9 5.4 reshape.59
  81.3 8.2 %copy.26 = bf16[4,32,8,768]{3,1,2,0:T(8,128)(2,1)S(1)} copy(bf16[4,32,8,768]{1,0,3,2:T(4,128)(2,1)} %bitcast.45) | data formatting | bytes 3145728 | tf_op jit(solution)/shard_map/all_to_all | solution.py:163
  89.5 10.1 %convert_bitcast_fusion = bf16[8,1024,384]{1,2,0:T(8,128)(2,1)} fusion(bf16[1024,768,1]{1,0,2:T(8,128)(2,1)S(1)} %bitcast.50, s32[]{:T(128)S(6)} %select_n.50, bf16[768,8,384]{0,2,1:T(8,128)(2,1)} %bitcast.47), kind=kOutput, calls=%fused_computation.4 | convolution fusion | flops 4837343232 | bytes 12582916 | tf_op jit(solution)/shard_map/td,dzb->ztb/dot_general | solution.py:167
  99.6 1.1 copy-done.4
  100.7 0.1 copy.32
  100.8 0.6 fusion.13
  101.4 0.1 copy.28
  101.5 29.9 %all_to_all.35 = bf16[4,32,8,384]{3,1,0,2:T(8,128)(2,1)S(1)} all-to-all(bf16[4,32,8,384]{3,1,0,2:T(8,128)(2,1)S(1)} %copy.28), channel_id=1, replica_groups=mesh['dp'=8,'section'=16,'mp'=2] {'dp'}, dimensions={2} | all-to-all | bytes 1572864 | tf_op jit(solution)/shard_map/all_to_all | solution.py:172
  131.4 0.1 copy.29
  131.5 54.5 %reduce-scatter.2.cloned.1.call-done = bf16[1,1024,384]{1,2,0:T(8,128)(2,1)} async-done(((bf16[8,1024,384]{1,2,0:T(8,128)(2,1)}), bf16[1,1024,384]{1,2,0:T(8,128)(2,1)}) %reduce-scatter.2.cloned.1.call-update) | async-done | bytes 786448 | tf_op jit(solution)/shard_map/reduce_scatter | solution.py:168
  186.0 2.5 copy.27
  188.6 2.3 fusion.10.slope
  190.9 2.3 copy-done.1
  193.2 482.5 %shard_map.59 = (bf16[32,32,3072]{2,1,0:T(8,128)(2,1)S(1)}, bf16[32,32,384]{2,1,0:T(8,128)(2,1)S(1)}) custom-call(bf16[768,3072]{1,0:T(8,128)(2,1)S(1)} %bitcast.40, f32[32,32,384]{2,1,0:T(8,128)S(1)} %fusion.10.slope, bf16[32,32,384]{2,1,0:T(8,128)(2,1)S(1)} %bitcast.41), custom_call_target="tpu_custom_call" | custom-call | flops 4831838208 | bytes 11010048 | tf_op jit(solution)/shard_map/pallas_call | solution.py:118
  675.7 2.7 copy-done.2
  678.4 21.0 %collective-permute-done = bf16[1024,384]{1,0:T(8,128)(2,1)S(1)} collective-permute-done((bf16[1024,384]{1,0:T(8,128)(2,1)S(1)}, bf16[1024,384]{1,0:T(8,128)(2,1)S(1)}, u32[]{:S(2)}, u32[]{:S(2)}) %collective-permute-start) | collective-permute-done | bytes 786464 | tf_op jit(solution)/shard_map/ppermute | solution.py:176
  699.4 1.0 copy.30
  700.4 3.7 all-to-all-start.2
  704.2 9.1 %fusion.3 = bf16[1,768,3072]{2,1,0:T(8,128)(2,1)} fusion(bf16[1024,768]{1,0:T(8,128)(2,1)} %bitcast.51, bf16[1024,3072]{1,0:T(8,128)(2,1)} %bitcast.43), kind=kOutput, calls=%fused_computation.7 | convolution fusion | flops 4836556800 | bytes 12582912 | tf_op jit(solution)/shard_map/dot_general | solution.py:181
  713.2 5.8 all-to-all-done.2
  719.1 0.3 fusion.12
  719.4 0.5 copy.31
  719.9 1.2 broadcast_in_dim_reshape.3
  (12 shorter events, 0.1 us)
Async XLA Ops:
  7.2 1.4 copy-start
  28.6 47.3 %all-to-all-start = ((bf16[8,2,49152]{2,1,0:T(2,128)(2,1)}), bf16[8,2,49152]{2,1,0:T(2,128)(2,1)S(1)}, u32[]{:S(2)}, u32[]{:S(2)}) async-start(bf16[8,2,49152]{2,1,0:T(2,128)(2,1)} %reshape.58), calls=%async_computation | async-start | bytes 3145728 | tf_op jit(solution)/shard_map/all_to_all | solution.py:163
  37.6 148.4 %reduce-scatter.2.cloned.1.call-start = ((), (), s32[]{:S(2)}) async-start(), calls=%async_computation.4 | async-start | bytes 7077888 | tf_op jit(solution)/shard_map/reduce_scatter | solution.py:168
  89.4 10.1 %copy-start.3 = (bf16[4,32,8,768]{3,1,2,0:T(8,128)(2,1)}, bf16[4,32,8,768]{3,1,2,0:T(8,128)(2,1)S(1)}, u32[]{:S(2)}) copy-start(bf16[4,32,8,768]{3,1,2,0:T(8,128)(2,1)S(1)} %copy.26) | copy-start | bytes 4718596
  99.6 1.1 copy-start.4
  190.9 2.3 copy-start.1
  675.7 2.7 copy-start.2
  678.4 21.0 %collective-permute-start = (bf16[1024,384]{1,0:T(8,128)(2,1)S(1)}, bf16[1024,384]{1,0:T(8,128)(2,1)S(1)}, u32[]{:S(2)}, u32[]{:S(2)}) collective-permute-start(bf16[1024,384]{1,0:T(8,128)(2,1)S(1)} %bitcast.42), channel_id=1, source_target_pairs={{0,2},{2,4},{4,6},{6,8},{8,10},{10,12},{12,14},{14,16},{16,18},{18... | collective-permute-start | bytes 2359304 | tf_op jit(solution)/shard_map/ppermute | solution.py:176
  700.4 18.7 %all-to-all-start.2 = ((bf16[4,8,32,384]{3,2,0,1:T(8,128)(2,1)}), bf16[4,8,32,384]{3,2,0,1:T(8,128)(2,1)S(1)}, u32[]{:S(2)}, u32[]{:S(2)}) async-start(bf16[4,8,32,384]{3,2,0,1:T(8,128)(2,1)} %copy.30), calls=%async_computation.3 | async-start | bytes 1572864 | tf_op jit(solution)/shard_map/all_to_all | solution.py:177
Sparse Core Ops, SparseCore 0:
  99.7 86.2 reduce-scatter.1

commit v2 on v1

v2 whole, which is shorter than its diff:
```python
import jax
import jax.numpy as jnp
from jax import lax
from jax.experimental import pallas as pl
from jax.experimental.pallas import tpu as pltpu
from jax.sharding import PartitionSpec as P

MESH = pl.DeviceIdType.MESH
LAG = 1


def gelu_slope(value):
    inner = 0.7978845608 * (value + 0.044715 * value * value * value)
    tangent = jnp.tanh(inner)
    return 0.5 * (1.0 + tangent) + 0.5 * value * (1.0 - tangent * tangent) * 0.7978845608 * (
        1.0 + 3.0 * 0.044715 * value * value
    )


def send(src, dst, send_sem, recv_sem, device):
    pltpu.make_async_remote_copy(
        src_ref=src, dst_ref=dst, send_sem=send_sem, recv_sem=recv_sem, device_id=device, device_id_type=MESH
    ).start()


def await_bytes(ref, sem):
    pltpu.make_async_copy(ref, ref, sem).wait()


def turn_of(m, nz):
    return (nz // 4) * (1 - 2 * m)


def prepare_kernel(x_own, w, x_out, slope, x, ring, sent, x_sem, x_sent, y_sem, y_sent, own_sem, ring_sem, ring_sent, flush_sem):
    nz = lax.axis_size("dp")
    z, s, m = lax.axis_index("dp"), lax.axis_index("section"), lax.axis_index("mp")
    micro, _, rows, depth = x.shape
    block = slope.shape[-1]
    pair = micro // 2
    steps = sorted(range(1, nz), key=lambda k: min(k, nz - k))
    partner = (z, s, 1 - m)
    mine = pl.ds(m * pair, pair)
    theirs = pl.ds((1 - m) * pair, pair)

    barrier = pltpu.get_barrier_semaphore()
    for step in steps:
        pl.semaphore_signal(barrier, inc=1, device_id=(lax.rem(z + step, nz), s, m), device_id_type=MESH)
    pl.semaphore_signal(barrier, inc=1, device_id=partner, device_id_type=MESH)
    pl.semaphore_wait(barrier, nz)

    def piece(owner):
        return x_own.at[mine, :, pl.ds(pl.multiple_of(owner * depth, depth), depth)]

    own = pltpu.make_async_copy(piece(z), x.at[mine, z], own_sem)
    own.start()
    for step in steps[::-1]:
        owner = lax.rem(z + step, nz)
        send(piece(owner), x.at[mine, z], x_sent.at[step], x_sem.at[step], (owner, s, m))
    send(piece(z), x.at[mine, z], y_sent.at[0], y_sem.at[0], partner)
    for step in steps:
        origin = lax.rem(z + nz - step, nz)
        await_bytes(x.at[mine, origin], x_sem.at[step])
        send(x.at[mine, origin], x.at[mine, origin], y_sent.at[step], y_sem.at[step], partner)
    own.wait()
    for step in range(nz):
        await_bytes(x.at[theirs, lax.rem(z + nz - step, nz)], y_sem.at[step])
    flush = pltpu.make_async_copy(x, x_out, flush_sem)
    flush.start()

    def partial(t, q):
        owner = lax.rem(z + 2 * nz - 1 - t, nz) if q < pair else lax.rem(z + 1 + t, nz)
        at = lax.rem(owner + nz + turn_of(m, nz), nz) * block
        return jnp.dot(
            x[q].reshape(nz * rows, depth),
            w[:, pl.ds(pl.multiple_of(at, block), block)],
            preferred_element_type=jnp.float32,
        )

    def pass_on(t, q, value):
        sent[t, q] = value.astype(jnp.bfloat16)
        to = lax.rem(z + 1, nz) if q < pair else lax.rem(z + nz - 1, nz)
        send(sent.at[t, q], ring.at[t, q], ring_sent.at[t, q], ring_sem.at[t, q], (to, s, m))

    order = [q // 2 + (q % 2) * pair for q in range(micro)]
    for q in order:
        pass_on(0, q, partial(0, q))

    def step_of(t, _):
        for q in order:
            value = partial(t, q)
            await_bytes(ring.at[t - 1, q], ring_sem.at[t - 1, q])
            pass_on(t, q, value + ring[t - 1, q].astype(jnp.float32))
        return 0

    lax.fori_loop(1, nz - 1, step_of, 0)
    for q in order:
        value = partial(nz - 1, q)
        await_bytes(ring.at[nz - 2, q], ring_sem.at[nz - 2, q])
        slope[q] = gelu_slope(value + ring[nz - 2, q].astype(jnp.float32))

    flush.wait()
    for step in steps:
        await_bytes(x.at[mine, z], x_sent.at[step])
    for step in range(nz):
        await_bytes(x.at[mine, z], y_sent.at[step])

    def drain(t, _):
        for q in range(micro):
            await_bytes(sent.at[t, q], ring_sent.at[t, q])
        return 0

    lax.fori_loop(0, nz - 1, drain, 0)


def prepare(x_own, w, cid=0):
    nz = lax.axis_size("dp")
    micro, rows, width = x_own.shape
    depth, half = w.shape
    block = half // nz
    dma = pltpu.SemaphoreType.DMA
    return pl.pallas_call(
        prepare_kernel,
        out_shape=(
            jax.ShapeDtypeStruct((micro, nz, rows, depth), jnp.bfloat16),
            jax.ShapeDtypeStruct((micro, nz * rows, block), jnp.float32),
        ),
        in_specs=[pl.BlockSpec(memory_space=pltpu.VMEM)] * 2,
        out_specs=(pl.BlockSpec(memory_space=pl.ANY), pl.BlockSpec(memory_space=pltpu.VMEM)),
        scratch_shapes=[
            pltpu.VMEM((micro, nz, rows, depth), jnp.bfloat16),
            pltpu.VMEM((nz - 1, micro, nz * rows, block), jnp.bfloat16),
            pltpu.VMEM((nz - 1, micro, nz * rows, block), jnp.bfloat16),
            dma((nz,)),
            dma((nz,)),
            dma((nz,)),
            dma((nz,)),
            dma,
            dma((nz - 1, micro)),
            dma((nz - 1, micro)),
            dma,
        ],
        compiler_params=pltpu.CompilerParams(
            collective_id=cid, has_side_effects=True, vmem_limit_bytes=44 * 1024 * 1024
        ),
        cost_estimate=pl.CostEstimate(
            flops=2 * micro * nz * rows * depth * half,
            bytes_accessed=2 * depth * half,
            transcendentals=0,
        ),
    )(x_own, w)


def relay_kernel(w, slope, top, hidden_out, grad_out, h, inbox, carried, product, back, in_sem, h_sem, out_sem, copy_sem, flush_sem, back_sent, back_sem, top_sent, top_sem):
    nz, ns = lax.axis_size("dp"), lax.axis_size("section")
    z, s, m = lax.axis_index("dp"), lax.axis_index("section"), lax.axis_index("mp")
    chunks, rows, columns = h.shape
    micro = chunks // nz
    block = columns // nz
    above, below = lax.rem(s + 1, ns), lax.rem(s + ns - 1, ns)
    is_top = s == ns - 1

    def place(owner):
        return pl.ds(pl.multiple_of(lax.rem(owner + nz + turn_of(m, nz), nz) * block, block), block)

    source = m * (nz // 2) + lax.rem(z + nz + turn_of(m, nz), nz) // 2
    to_m = z // (nz // 2)
    first = 2 * lax.rem(z, nz // 2) + nz - turn_of(to_m, nz)
    owners = [lax.rem(first, nz), lax.rem(first + 1, nz)]
    mine = place(z)

    barrier = pltpu.get_barrier_semaphore()
    for step in range(1, nz):
        pl.semaphore_signal(barrier, inc=1, device_id=(lax.rem(z + step, nz), s, m), device_id_type=MESH)
    for step in range(nz):
        pl.semaphore_signal(barrier, inc=1, device_id=(lax.rem(z + step, nz), below, m), device_id_type=MESH)
    pl.semaphore_signal(barrier, inc=1, device_id=(z, above, m), device_id_type=MESH)
    for part in range(2):
        pl.semaphore_signal(barrier, inc=1, device_id=(source, above, part), device_id_type=MESH)
    pl.semaphore_wait(barrier, 2 * nz + 2)

    @pl.when(is_top)
    def _():
        def spread(q, _):
            for step in range(1, nz):
                owner = lax.rem(z + step, nz)
                send(top.at[q, :, place(owner)], carried.at[q * nz + z], top_sent.at[q], top_sem.at[q], (owner, s, m))
            carried[q * nz + z] = top[q, :, mine]
            return 0

        lax.fori_loop(0, micro, spread, 0)

    def received(c):
        await_bytes(inbox.at[c], in_sem.at[c])
        unit_sum = inbox[c, 0].astype(jnp.float32) + inbox[c, 1].astype(jnp.float32)
        return (inbox[c, 2].astype(jnp.float32) + unit_sum).astype(jnp.bfloat16)

    def send_back(c):
        q, d = c // nz, lax.rem(c, nz)
        send(carried.at[c], back.at[q, :, mine], back_sent, back_sem, (d, above, m))

    def share(c, owner, step, sem):
        at = place(owner)
        send(h.at[c, :, at], h.at[c, :, at], copy_sem.at[c], sem.at[c], (lax.rem(z + nz + step, nz), s, m))

    def publish(c):
        @pl.when(is_top)
        def _():
            @pl.when(lax.rem(c, nz) == 0)
            def _():
                await_bytes(carried.at[pl.ds(0, nz - 1)], top_sem.at[c // nz])

        @pl.when(jnp.logical_not(is_top))
        def _():
            carried[c] = received(c)

        h[c, :, mine] = (carried[c].astype(jnp.float32) * slope[c]).astype(jnp.bfloat16)
        for step in sorted(range(1, nz), key=lambda k: -min(k, nz - k)):
            share(c, z, step, h_sem)
        send(carried.at[c], inbox.at[c, 2], out_sem.at[c], in_sem.at[c], (z, below, m))

    def multiply(c):
        await_bytes(h.at[c, :, pl.ds(0, (nz - 1) * block)], h_sem.at[c])
        value = jnp.dot(h[c], w[...], preferred_element_type=jnp.float32).astype(jnp.bfloat16)
        for part in range(2):
            product[c, part] = value[:, part * block : (part + 1) * block]
            send(product.at[c, part], inbox.at[c, m], out_sem.at[c], in_sem.at[c], (owners[part], below, to_m))
        pltpu.make_async_copy(h.at[c], hidden_out.at[c], flush_sem.at[c]).start()

    def advance(i, _):
        @pl.when(i < chunks)
        def _():
            publish(i)

        @pl.when(i >= LAG)
        def _():
            multiply(i - LAG)

        return 0

    lax.fori_loop(0, chunks + LAG, advance, 0)

    @pl.when(jnp.logical_not(is_top))
    def _():
        def later(c, _):
            send_back(c)
            return 0

        lax.fori_loop(0, chunks, later, 0)

    @pl.when(is_top)
    def _():
        for q in range(micro):
            await_bytes(carried.at[pl.ds(0, nz - 1)], top_sent.at[q])

        def last(c, _):
            await_bytes(inbox.at[c], out_sem.at[c])
            carried[c] = received(c)
            send_back(c)
            return 0

        lax.fori_loop(0, chunks, last, 0)

    def drain(c, _):
        await_bytes(h.at[c, :, pl.ds(0, (nz - 1) * block)], copy_sem.at[c])

        @pl.when(jnp.logical_not(is_top))
        def _():
            await_bytes(inbox.at[c], out_sem.at[c])

        await_bytes(h.at[c], flush_sem.at[c])
        return 0

    lax.fori_loop(0, chunks, drain, 0)
    await_bytes(back, back_sem)
    grad_out[...] = back[...]
    await_bytes(back, back_sent)


def relay(w, slope, top, cid=1):
    columns, depth = w.shape
    micro, rows, _ = top.shape
    block = slope.shape[-1]
    tokens = slope.shape[0] * slope.shape[1]
    chunks = tokens // rows
    dma = pltpu.SemaphoreType.DMA
    return pl.pallas_call(
        relay_kernel,
        out_shape=(
            jax.ShapeDtypeStruct((chunks, rows, columns), jnp.bfloat16),
            jax.ShapeDtypeStruct((micro, rows, columns), jnp.bfloat16),
        ),
        in_specs=[pl.BlockSpec(memory_space=pltpu.VMEM)] * 3,
        out_specs=(pl.BlockSpec(memory_space=pl.ANY), pl.BlockSpec(memory_space=pltpu.VMEM)),
        scratch_shapes=[
            pltpu.VMEM((chunks, rows, columns), jnp.bfloat16),
            pltpu.VMEM((chunks, 3, rows, block), jnp.bfloat16),
            pltpu.VMEM((chunks, rows, block), jnp.bfloat16),
            pltpu.VMEM((chunks, 2, rows, block), jnp.bfloat16),
            pltpu.VMEM((micro, rows, columns), jnp.bfloat16),
            dma((chunks,)),
            dma((chunks,)),
            dma((chunks,)),
            dma((chunks,)),
            dma((chunks,)),
            dma,
            dma,
            dma((micro,)),
            dma((micro,)),
        ],
        compiler_params=pltpu.CompilerParams(
            collective_id=cid, has_side_effects=True, vmem_limit_bytes=40 * 1024 * 1024
        ),
        cost_estimate=pl.CostEstimate(
            flops=2 * tokens * depth * columns,
            bytes_accessed=2 * (depth + tokens) * columns,
            transcendentals=0,
        ),
    )(w, slope.reshape(chunks, rows, block), top)


def on_device(stash, w_mix, top_grad, order):
    micro = stash.shape[1]
    weight = w_mix[0]
    depth, half = weight.shape

    series = jnp.arange(micro, dtype=jnp.int32)
    match = (order[0][None, :] == series[:, None]).astype(jnp.int32)
    slot_table = jnp.sum(series[None, :] * match, axis=1)
    x_own = jnp.take(stash[0], slot_table, axis=0)
    x, slope = prepare(x_own, weight)
    x = x.reshape(-1, depth)
    hidden, input_grad = relay(weight.T, slope, top_grad)
    grad_mix = x.shape[0] ** (-0.5) * lax.dot_general(
        x, hidden.reshape(-1, half), (((0,), (0,)), ((), ())), preferred_element_type=jnp.float32
    )
    return (input_grad[None], grad_mix.astype(jnp.bfloat16)[None])


def solution(mesh):
    in_specs = (
        P("section", None, "dp", None),
        P("section", "dp", "mp"),
        P(None, "dp", "mp"),
        P("section", None),
    )
    out_specs = (P("section", None, "dp", "mp"), P("section", "dp", "mp"))
    return jax.shard_map(
        on_device, mesh=mesh, in_specs=in_specs, out_specs=out_specs, check_vma=False
    )
```

time: 742 us -> 546 us (0.74); the launches traced: 728 us -> 546 us
  waiting for transfers between devices: 113 us -> 0 us
  Pallas kernels: 482 us -> 519 us
  local copies, waits for them, and re-layouts: 51 us -> 18 us
  blocking collectives: 29.9 us -> 0 us
  between operations: 14.2 us -> 0.71 us
  starting transfers between devices: 12.8 us -> 0 us
  matrix products: 19.2 us -> 6.8 us
    pallas_call x0 -> x1, Pallas kernels: none -> 104 us  [prepare(): pl.pallas_call(prepare_kernel, out_shape=(jax.ShapeDtypeStruct((micro, nz...]
    pallas_call x1, Pallas kernels: 482 us -> 415 us  [relay(): pl.pallas_call(relay_kernel, out_shape=(jax.ShapeDtypeStruct((chunks, row...]
    reduce_scatter x1 -> x0, waiting for transfers between devices: 54.5 us -> none  [on_device(): lax.psum_scatter(partial.astype(jnp.bfloat16), 'dp', scatter_dimension=0,...]
    all_to_all x2 -> x0, waiting for transfers between devices: 37.4 us -> none  [the longest x1 31.6 us: on_device(): lax.all_to_all(x_own, 'dp', split_axis=2, concat_axis=1, tiled=True)]
    all_to_all x1 -> x0, blocking collectives: 29.9 us -> none  [on_device(): lax.all_to_all(top_blocks, 'dp', split_axis=2, concat_axis=1, tiled=True)]
    ppermute x1 -> x0, waiting for transfers between devices: 21 us -> none  [on_device(): grad = lax.ppermute(grad, 'section', [(i, (i + 1) % ns) for i in range(ns)])]
    all_to_all x2 -> x0, starting transfers between devices: 12.7 us -> none  [the longest x1 9.01 us: on_device(): lax.all_to_all(x_own, 'dp', split_axis=2, concat_axis=1, tiled=True)]
    dot_general x2 -> x1, matrix products: 19.2 us -> 6.8 us  [on_device(): lax.dot_general(x, hidden.reshape(-1, half), (((0,), (0,)), ((), ())), pr...]
  transfers between devices with their start and end apart: 4 -> 0, of which waited for: 4 -> 0; matrix products, arithmetic and copies ran while one was open for 2% -> 0% of each run, Pallas kernels for 0% -> 0%
where the time goes in v2:
time: 546 us
  Pallas kernels  519 us (95%)
  local copies, waits for them, and re-layouts  18 us (3%)
  matrix products  6.8 us (1%)
    pallas_call x1, Pallas kernels, relay(): pl.pallas_call(relay_kernel, out_shape=(jax.ShapeDtypeStruct((chunks, row...  415 us
    pallas_call x1, Pallas kernels, prepare(): pl.pallas_call(prepare_kernel, out_shape=(jax.ShapeDtypeStruct((micro, nz...  104 us
    unnamed x18, local copies, waits for them, and re-layouts  17.3 us

profile of v2, /device:TPU:1, one launch (start us, length us, event | category | flops | bytes accessed | tf_op | source)
XLA Modules:
  0.0 545.7 jit_solution(4496785555306962309)
XLA Ops:
  0.6 0.0 copy-start
  0.6 1.4 copy-done
  2.0 0.8 select_reduce_fusion
  2.8 0.6 gather_fusion
  3.5 0.2 broadcast_select_fusion.x_own
  3.7 0.0 copy-start.1
  3.7 2.3 copy-done.1
  6.1 104.1 %shard_map.59 = (bf16[4,8,32,768]{3,2,1,0:T(8,128)(2,1)S(1)}, f32[4,256,384]{2,1,0:T(8,128)S(1)}) custom-call(bf16[4,32,6144]{2,1,0:T(8,128)(2,1)S(1)} %broadcast_select_fusion.x_own, bf16[768,3072]{1,0:T(8,128)(2,1)S(1)} %bitcast.19), custom_call_target="tpu_custom_call" | custom-call | flops 4831838208 | bytes 4718592 | tf_op jit(solution)/shard_map/pallas_call | solution.py:121
  110.1 0.0 copy-start.4
  110.1 1.1 copy-done.4
  111.3 0.0 copy-start.6
  111.3 1.2 copy-done.6
  112.4 0.0 copy-start.3
  112.4 6.7 %copy.8 = bf16[1,768,3072]{1,2,0:T(8,128)(2,1)} copy(bf16[1,768,3072]{2,1,0:T(8,128)(2,1)} %param.5) | data formatting | bytes 9437184 | tf_op args[1]
  119.1 0.0 copy-done.3
  119.1 0.0 copy-start.2
  119.1 2.3 copy-done.2
  121.5 0.0 copy-start.7
  121.5 1.4 copy-done.7
  122.9 0.0 copy-start.5
  122.9 415.1 %shard_map.60 = (bf16[32,32,3072]{2,1,0:T(8,128)(2,1)S(1)}, bf16[4,32,3072]{2,1,0:T(8,128)(2,1)S(1)}) custom-call(bf16[3072,768]{1,0:T(8,128)(2,1)S(1)} %bitcast.20, f32[32,32,384]{2,1,0:T(8,128)S(1)} %bitcast.24, bf16[4,32,3072]{2,1,0:T(8,128)(2,1)S(1)} %copy-done.3), custom_call_target="tpu_custom_call" | custom-call | flops 4831838208 | bytes 11010048 | tf_op jit(solution)/shard_map/pallas_call | solution.py:286
  538.0 0.0 copy-done.5
  538.0 6.8 %fusion = bf16[1,768,3072]{2,1,0:T(8,128)(2,1)} fusion(bf16[1024,768]{1,0:T(8,128)(2,1)S(1)} %bitcast.23, bf16[1024,3072]{1,0:T(8,128)(2,1)S(1)} %bitcast.22), kind=kOutput, calls=%fused_computation.2 | convolution fusion | flops 4836556800 | bytes 12582912 | tf_op jit(solution)/shard_map/dot_general | solution.py:333
  544.8 0.9 copy.12
  (3 shorter events, 0.0 us)
Async XLA Ops:
  0.6 1.4 copy-start
  3.7 2.3 copy-start.1
  110.1 1.1 copy-start.4
  111.3 1.2 copy-start.6
  112.4 6.7 %copy-start.3 = (bf16[4,32,3072]{2,1,0:T(8,128)(2,1)S(1)}, bf16[4,32,3072]{2,1,0:T(8,128)(2,1)}, u32[]{:S(2)}) copy-start(bf16[4,32,3072]{2,1,0:T(8,128)(2,1)} %top.1) | copy-start | bytes 2359300
  119.1 2.3 copy-start.2
  121.5 1.4 copy-start.7
  122.9 415.2 %copy-start.5 = (bf16[4,8,32,768]{3,2,1,0:T(8,128)(2,1)S(1)}, bf16[4,8,32,768]{3,2,1,0:T(8,128)(2,1)}, u32[]{:S(2)}) copy-start(bf16[4,8,32,768]{3,2,1,0:T(8,128)(2,1)} %copy-done.4) | copy-start | bytes 4718596

commit v3 on v2

v3 whole, which is shorter than its diff:
```python
import jax
import jax.numpy as jnp
from jax import lax
from jax.experimental import pallas as pl
from jax.experimental.pallas import tpu as pltpu
from jax.sharding import PartitionSpec as P

MESH = pl.DeviceIdType.MESH
LAG = 1


def gelu_slope(value):
    inner = 0.7978845608 * (value + 0.044715 * value * value * value)
    tangent = jnp.tanh(inner)
    return 0.5 * (1.0 + tangent) + 0.5 * value * (1.0 - tangent * tangent) * 0.7978845608 * (
        1.0 + 3.0 * 0.044715 * value * value
    )


def send(src, dst, send_sem, recv_sem, device):
    pltpu.make_async_remote_copy(
        src_ref=src, dst_ref=dst, send_sem=send_sem, recv_sem=recv_sem, device_id=device, device_id_type=MESH
    ).start()


def await_bytes(ref, sem):
    pltpu.make_async_copy(ref, ref, sem).wait()


def turn_of(m, nz):
    return (nz // 4) * (1 - 2 * m)


def layer_kernel(x_own, w, top, x_out, hidden_out, grad_out, x, ring, sent, w_t, slope_in, h, inbox, carried, shared, product, slope, back, in_sem, h_sem, out_sem, copy_sem, flush_sem, back_sent, back_sem, top_sent, top_sem, slope_sent, slope_sem, x_sem, x_sent, y_sem, y_sent, own_sem, ring_sem, ring_sent, x_flush_sem):
    nz, ns = lax.axis_size("dp"), lax.axis_size("section")
    z, s, m = lax.axis_index("dp"), lax.axis_index("section"), lax.axis_index("mp")
    chunks, rows, columns = h.shape
    micro = chunks // nz
    block = columns // nz
    depth = x.shape[-1]
    pair = micro // 2
    steps = sorted(range(1, nz), key=lambda k: min(k, nz - k))
    partner = (z, s, 1 - m)
    kept = pl.ds(m * pair, pair)
    given = pl.ds((1 - m) * pair, pair)
    above, below = lax.rem(s + 1, ns), lax.rem(s + ns - 1, ns)
    is_top = s == ns - 1

    to_m = z // (nz // 2)
    own = 2 * lax.rem(z, nz // 2) + m
    in_column = to_m == m

    def place(number):
        return pl.ds(pl.multiple_of(number * block, block), block)

    def owner_of(number):
        return (m * (nz // 2) + number // 2, s, lax.rem(number, 2))

    def each_other(step, call):
        if step:
            call(step)
        else:
            pl.when(jnp.logical_not(in_column))(lambda: call(step))

    barrier = pltpu.get_barrier_semaphore()

    def greet(device):
        pl.semaphore_signal(barrier, inc=1, device_id=device, device_id_type=MESH)

    for step in range(nz):
        each_other(step, lambda k: greet(owner_of(lax.rem(own + k, nz))))
        each_other(step, lambda k: greet((lax.rem(z + k, nz), s, to_m)))
        greet((m * (nz // 2) + step // 2, below, step % 2))
    for step in steps:
        greet((lax.rem(z + step, nz), s, m))
    greet(partner)
    greet((z, above, 0))
    greet((z, above, 1))
    pl.when(in_column)(lambda: pl.semaphore_wait(barrier, 4 * nz))
    pl.when(jnp.logical_not(in_column))(lambda: pl.semaphore_wait(barrier, 4 * nz + 2))

    mine = place(own)
    number = lax.rem(z + nz + turn_of(m, nz), nz)
    at_home = jnp.logical_and(in_column, number == own)

    def piece(owner):
        return x_own.at[kept, :, pl.ds(pl.multiple_of(owner * depth, depth), depth)]

    own_copy = pltpu.make_async_copy(piece(z), x.at[kept, z], own_sem)
    own_copy.start()
    for step in steps[::-1]:
        owner = lax.rem(z + step, nz)
        send(piece(owner), x.at[kept, z], x_sent.at[step], x_sem.at[step], (owner, s, m))
    send(piece(z), x.at[kept, z], y_sent.at[0], y_sem.at[0], partner)

    @pl.when(is_top)
    def _():
        def spread(q, _):
            def give(step):
                to = lax.rem(own + step, nz)
                send(top.at[q, :, place(to)], carried.at[q * nz + z], top_sent.at[q], top_sem.at[q], owner_of(to))

            for step in range(nz):
                each_other(step, give)

            @pl.when(in_column)
            def _():
                carried[q * nz + z] = top[q, :, mine]

            return 0

        lax.fori_loop(0, micro, spread, 0)

    def transpose(k, _):
        at = pl.ds(pl.multiple_of(k * block, block), block)
        w_t[at, :] = w[:, at].T
        return 0

    lax.fori_loop(0, nz, transpose, 0)

    for step in steps:
        origin = lax.rem(z + nz - step, nz)
        await_bytes(x.at[kept, origin], x_sem.at[step])
        send(x.at[kept, origin], x.at[kept, origin], y_sent.at[step], y_sem.at[step], partner)
    own_copy.wait()
    for step in range(nz):
        await_bytes(x.at[given, lax.rem(z + nz - step, nz)], y_sem.at[step])
    x_flush = pltpu.make_async_copy(x, x_out, x_flush_sem)
    x_flush.start()

    def partial(t, q):
        owner = lax.rem(z + 2 * nz - 1 - t, nz) if q < pair else lax.rem(z + 1 + t, nz)
        at = lax.rem(owner + nz + turn_of(m, nz), nz) * block
        return jnp.dot(
            x[q].reshape(nz * rows, depth),
            w[:, pl.ds(pl.multiple_of(at, block), block)],
            preferred_element_type=jnp.float32,
        )

    def pass_on(t, q, value):
        sent[t, q] = value.astype(jnp.bfloat16)
        to = lax.rem(z + 1, nz) if q < pair else lax.rem(z + nz - 1, nz)
        send(sent.at[t, q], ring.at[t, q], ring_sent.at[t, q], ring_sem.at[t, q], (to, s, m))

    def local_slope(q):
        part = pl.ds(q * nz, nz)
        return pltpu.make_async_copy(slope_in.at[part], slope.at[part], slope_sem.at[q])

    order = [q // 2 + (q % 2) * pair for q in range(micro)]
    for q in order:
        pass_on(0, q, partial(0, q))

    def step_of(t, _):
        for q in order:
            value = partial(t, q)
            await_bytes(ring.at[t - 1, q], ring_sem.at[t - 1, q])
            pass_on(t, q, value + ring[t - 1, q].astype(jnp.float32))
        return 0

    lax.fori_loop(1, nz - 1, step_of, 0)
    for q in order:
        value = partial(nz - 1, q)
        await_bytes(ring.at[nz - 2, q], ring_sem.at[nz - 2, q])
        value = gelu_slope(value + ring[nz - 2, q].astype(jnp.float32)).astype(jnp.bfloat16)
        part = pl.ds(q * nz, nz)
        slope_in[part] = value.reshape(nz, rows, block)
        pl.when(at_home)(lambda: local_slope(q).start())

        @pl.when(jnp.logical_not(at_home))
        def _():
            send(slope_in.at[part], slope.at[part], slope_sent.at[q], slope_sem.at[q], owner_of(number))

    def await_blocks(ref, sem):
        pl.when(in_column)(lambda: await_bytes(ref.at[pl.ds(0, nz - 1)], sem))
        pl.when(jnp.logical_not(in_column))(lambda: await_bytes(ref.at[pl.ds(0, nz)], sem))

    def received(c):
        await_bytes(inbox.at[c], in_sem.at[c])
        return (inbox[c, 0].astype(jnp.float32) + inbox[c, 1].astype(jnp.float32)).astype(jnp.bfloat16)

    def send_back(c):
        q, d = c // nz, lax.rem(c, nz)
        send(carried.at[c], back.at[q, :, mine], back_sent, back_sem, (d, above, to_m))

    def publish(c):
        @pl.when(lax.rem(c, nz) == 0)
        def _():
            await_bytes(slope.at[pl.ds(c, nz)], slope_sem.at[c // nz])

            @pl.when(is_top)
            def _():
                await_blocks(carried, top_sem.at[c // nz])

        @pl.when(jnp.logical_not(is_top))
        def _():
            carried[c] = received(c)

        value = (carried[c].astype(jnp.float32) * slope[c].astype(jnp.float32)).astype(jnp.bfloat16)
        shared[c] = value

        def share(step):
            send(shared.at[c], h.at[c, :, mine], copy_sem.at[c], h_sem.at[c, own // 2], (lax.rem(z + step, nz), s, to_m))

        for step in sorted(range(nz), key=lambda k: -min(k, nz - k)):
            each_other(step, share)

        @pl.when(in_column)
        def _():
            h[c, :, mine] = value

    sources = nz // 2
    nearest = jnp.where(in_column, z, z + 1)

    def multiply(c):
        total = None
        for k in range(sources):
            near = lax.rem(nearest + k, sources)
            if k:
                await_bytes(shared.at[pl.ds(0, 2)], h_sem.at[c, near])
            else:
                pl.when(in_column)(lambda: await_bytes(shared.at[0], h_sem.at[c, near]))
                pl.when(jnp.logical_not(in_column))(lambda: await_bytes(shared.at[pl.ds(0, 2)], h_sem.at[c, near]))
            at = pl.ds(pl.multiple_of(near * 2 * block, 2 * block), 2 * block)
            term = jnp.dot(h[c, :, at], w_t[at, :], preferred_element_type=jnp.float32)
            total = term if total is None else total + term
        for part in range(2):
            value = total[:, part * block : (part + 1) * block]
            value = value + jnp.where(m == part, carried[c].astype(jnp.float32), 0.0)
            product[c, part] = value.astype(jnp.bfloat16)
            send(product.at[c, part], inbox.at[c, m], out_sem.at[c], in_sem.at[c], (z, below, part))
        pltpu.make_async_copy(h.at[c], hidden_out.at[c], flush_sem.at[c]).start()

    def advance(i, _):
        @pl.when(i < chunks)
        def _():
            publish(i)

        @pl.when(i >= LAG)
        def _():
            multiply(i - LAG)

        return 0

    lax.fori_loop(0, chunks + LAG, advance, 0)

    @pl.when(jnp.logical_not(is_top))
    def _():
        def later(c, _):
            send_back(c)
            return 0

        lax.fori_loop(0, chunks, later, 0)

    @pl.when(is_top)
    def _():
        def last(c, _):
            await_bytes(inbox.at[c], out_sem.at[c])
            carried[c] = received(c)
            send_back(c)
            return 0

        lax.fori_loop(0, chunks, last, 0)
        for q in range(micro):
            await_blocks(shared, top_sent.at[q])

    def drain(c, _):
        await_blocks(shared, copy_sem.at[c])

        @pl.when(jnp.logical_not(is_top))
        def _():
            await_bytes(inbox.at[c], out_sem.at[c])

        await_bytes(h.at[c], flush_sem.at[c])
        return 0

    lax.fori_loop(0, chunks, drain, 0)

    @pl.when(jnp.logical_not(at_home))
    def _():
        for q in range(micro):
            await_bytes(slope.at[pl.ds(0, nz)], slope_sent.at[q])

    x_flush.wait()
    for step in steps:
        await_bytes(x.at[kept, z], x_sent.at[step])
    for step in range(nz):
        await_bytes(x.at[kept, z], y_sent.at[step])

    def drain_ring(t, _):
        for q in range(micro):
            await_bytes(sent.at[t, q], ring_sent.at[t, q])
        return 0

    lax.fori_loop(0, nz - 1, drain_ring, 0)

    await_bytes(back, back_sem)
    grad_out[...] = back[...]
    await_bytes(back, back_sent)


def layers(x_own, w, top, cid=0):
    nz = lax.axis_size("dp")
    micro, rows, _ = x_own.shape
    depth, columns = w.shape
    block = columns // nz
    chunks = micro * nz
    dma = pltpu.SemaphoreType.DMA

    def buffer(*shape):
        return pltpu.VMEM(shape, jnp.bfloat16)

    return pl.pallas_call(
        layer_kernel,
        out_shape=(
            jax.ShapeDtypeStruct((micro, nz, rows, depth), jnp.bfloat16),
            jax.ShapeDtypeStruct((chunks, rows, columns), jnp.bfloat16),
            jax.ShapeDtypeStruct((micro, rows, columns), jnp.bfloat16),
        ),
        in_specs=[pl.BlockSpec(memory_space=pltpu.VMEM)] * 3,
        out_specs=(
            pl.BlockSpec(memory_space=pl.ANY),
            pl.BlockSpec(memory_space=pl.ANY),
            pl.BlockSpec(memory_space=pltpu.VMEM),
        ),
        scratch_shapes=[
            buffer(micro, nz, rows, depth),
            buffer(nz - 1, micro, nz * rows, block),
            buffer(nz - 1, micro, nz * rows, block),
            buffer(columns, depth),
            buffer(chunks, rows, block),
            buffer(chunks, rows, columns),
            buffer(chunks, 2, rows, block),
            buffer(chunks, rows, block),
            buffer(chunks, rows, block),
            buffer(chunks, 2, rows, block),
            buffer(chunks, rows, block),
            buffer(micro, rows, columns),
            dma((chunks,)),
            dma((chunks, nz // 2)),
            dma((chunks,)),
            dma((chunks,)),
            dma((chunks,)),
            dma,
            dma,
            dma((micro,)),
            dma((micro,)),
            dma((micro,)),
            dma((micro,)),
            dma((nz,)),
            dma((nz,)),
            dma((nz,)),
            dma((nz,)),
            dma,
            dma((nz - 1, micro)),
            dma((nz - 1, micro)),
            dma,
        ],
        compiler_params=pltpu.CompilerParams(
            collective_id=cid, has_side_effects=True, vmem_limit_bytes=56 * 1024 * 1024
        ),
        cost_estimate=pl.CostEstimate(
            flops=4 * chunks * rows * depth * columns,
            bytes_accessed=4 * depth * columns,
            transcendentals=0,
        ),
    )(x_own, w, top)


def on_device(stash, w_mix, top_grad, order):
    micro = stash.shape[1]
    weight = w_mix[0]
    depth, half = weight.shape

    series = jnp.arange(micro, dtype=jnp.int32)
    match = (order[0][None, :] == series[:, None]).astype(jnp.int32)
    slot_table = jnp.sum(series[None, :] * match, axis=1)
    x_own = jnp.take(stash[0], slot_table, axis=0)
    x, hidden, input_grad = layers(x_own, weight, top_grad)
    x = x.reshape(-1, depth)
    grad_mix = x.shape[0] ** (-0.5) * lax.dot_general(
        x, hidden.reshape(-1, half), (((0,), (0,)), ((), ())), preferred_element_type=jnp.float32
    )
    return (input_grad[None], grad_mix.astype(jnp.bfloat16)[None])


def solution(mesh):
    in_specs = (
        P("section", None, "dp", None),
        P("section", "dp", "mp"),
        P(None, "dp", "mp"),
        P("section", None),
    )
    out_specs = (P("section", None, "dp", "mp"), P("section", "dp", "mp"))
    return jax.shard_map(
        on_device, mesh=mesh, in_specs=in_specs, out_specs=out_specs, check_vma=False
    )
```

time: 546 us -> 483 us (0.88)
  Pallas kernels: 519 us -> 468 us
  local copies, waits for them, and re-layouts: 18 us -> 2.94 us
    pallas_call x2 -> x1, Pallas kernels: 519 us -> 468 us  [layers(): pl.pallas_call(layer_kernel, out_shape=(jax.ShapeDtypeStruct((micro, nz,...]
    unnamed x18 -> x5, local copies, waits for them, and re-layouts: 17.3 us -> 2.29 us
where the time goes in v3:
time: 483 us
  Pallas kernels  468 us (97%)
  matrix products  9.15 us (2%)
    pallas_call x1, Pallas kernels, layers(): pl.pallas_call(layer_kernel, out_shape=(jax.ShapeDtypeStruct((micro, nz,...  468 us

profile of v3, /device:TPU:1, one launch (start us, length us, event | category | flops | bytes accessed | tf_op | source)
XLA Modules:
  0.0 483.0 jit_solution(1249004926629098735)
XLA Ops:
  0.6 0.0 copy-start
  0.6 1.4 copy-done
  2.0 0.8 select_reduce_fusion
  2.8 0.6 gather_fusion
  3.5 1.4 broadcast_select_fusion.x_own
  4.9 468.1 %shard_map.59 = (bf16[4,8,32,768]{3,2,1,0:T(8,128)(2,1)}, bf16[32,32,3072]{2,1,0:T(8,128)(2,1)}, bf16[4,32,3072]{2,1,0:T(8,128)(2,1)}) custom-call(bf16[4,32,6144]{2,1,0:T(8,128)(2,1)} %broadcast_select_fusion.x_own, bf16[768,3072]{1,0:T(8,128)(2,1)} %bitcast.16, bf16[4,32,3072]{2,1,0:T(8,128)(2,1)} %top.1), custom_call_target="tpu_custom_call" | custom-call | flops 9663676416 | bytes 9437184 | tf_op jit(solution)/shard_map/pallas_call | solution.py:312
  473.0 0.0 copy-start.1
  473.0 9.1 %fusion = bf16[1,768,3072]{2,1,0:T(8,128)(2,1)} fusion(bf16[1024,768]{1,0:T(8,128)(2,1)} %bitcast.19, bf16[1024,3072]{1,0:T(8,128)(2,1)} %bitcast.18), kind=kOutput, calls=%fused_computation.2 | convolution fusion | flops 4836556800 | bytes 12582912 | tf_op jit(solution)/shard_map/dot_general | solution.py:380
  482.1 0.0 copy-done.1
  482.1 0.9 copy.7
  (3 shorter events, 0.0 us)
Async XLA Ops:
  0.6 1.4 copy-start
  473.0 9.2 %copy-start.1 = (bf16[4,32,3072]{2,1,0:T(8,128)(2,1)S(1)}, bf16[4,32,3072]{2,1,0:T(8,128)(2,1)}, u32[]{:S(2)}) copy-start(bf16[4,32,3072]{2,1,0:T(8,128)(2,1)} %get-tuple-element.5) | copy-start | bytes 2359300

commit v4 on v3

--- a/solution.py
+++ b/solution.py
@@ -31,7 +31,7 @@
     return (nz // 4) * (1 - 2 * m)
 
 
-def layer_kernel(x_own, w, top, x_out, hidden_out, grad_out, x, ring, sent, w_t, slope_in, h, inbox, carried, shared, product, slope, back, in_sem, h_sem, out_sem, copy_sem, flush_sem, back_sent, back_sem, top_sent, top_sem, slope_sent, slope_sem, x_sem, x_sent, y_sem, y_sent, own_sem, ring_sem, ring_sent, x_flush_sem):
+def layer_kernel(x_own, w, top, mix_out, grad_out, x, x_t, mix, ring, sent, w_t, slope_in, h, inbox, carried, shared, product, slope, back, in_sem, h_sem, out_sem, copy_sem, mix_sem, back_sent, back_sem, top_sent, top_sem, slope_sent, slope_sem, x_sem, x_sent, y_sem, y_sent, own_sem, ring_sem, ring_sent):
     nz, ns = lax.axis_size("dp"), lax.axis_size("section")
     z, s, m = lax.axis_index("dp"), lax.axis_index("section"), lax.axis_index("mp")
     chunks, rows, columns = h.shape
@@ -41,8 +41,6 @@
     pair = micro // 2
     steps = sorted(range(1, nz), key=lambda k: min(k, nz - k))
     partner = (z, s, 1 - m)
-    kept = pl.ds(m * pair, pair)
-    given = pl.ds((1 - m) * pair, pair)
     above, below = lax.rem(s + 1, ns), lax.rem(s + ns - 1, ns)
     is_top = s == ns - 1
 
@@ -83,15 +81,20 @@
     number = lax.rem(z + nz + turn_of(m, nz), nz)
     at_home = jnp.logical_and(in_column, number == own)
 
-    def piece(owner):
-        return x_own.at[kept, :, pl.ds(pl.multiple_of(owner * depth, depth), depth)]
-
-    own_copy = pltpu.make_async_copy(piece(z), x.at[kept, z], own_sem)
-    own_copy.start()
-    for step in steps[::-1]:
-        owner = lax.rem(z + step, nz)
-        send(piece(owner), x.at[kept, z], x_sent.at[step], x_sem.at[step], (owner, s, m))
-    send(piece(z), x.at[kept, z], y_sent.at[0], y_sem.at[0], partner)
+    batches = [(m if k < pair else 1 - m) * pair + k % pair for k in range(micro)]
+
+    def piece(k, owner):
+        return x_own.at[batches[k], :, pl.ds(pl.multiple_of(owner * depth, depth), depth)]
+
+    def own_copy(k):
+        return pltpu.make_async_copy(piece(k, z), x.at[batches[k], z], own_sem.at[k])
+
+    for k in range(pair):
+        own_copy(k).start()
+        for step in steps[::-1]:
+            owner = lax.rem(z + step, nz)
+            send(piece(k, owner), x.at[batches[k], z], x_sent.at[k, step], x_sem.at[k, step], (owner, s, m))
+        send(piece(k, z), x.at[batches[k], z], y_sent.at[k, 0], y_sem.at[k, 0], partner)
 
     @pl.when(is_top)
     def _():
@@ -118,53 +121,58 @@
 
     lax.fori_loop(0, nz, transpose, 0)
 
-    for step in steps:
-        origin = lax.rem(z + nz - step, nz)
-        await_bytes(x.at[kept, origin], x_sem.at[step])
-        send(x.at[kept, origin], x.at[kept, origin], y_sent.at[step], y_sem.at[step], partner)
-    own_copy.wait()
-    for step in range(nz):
-        await_bytes(x.at[given, lax.rem(z + nz - step, nz)], y_sem.at[step])
-    x_flush = pltpu.make_async_copy(x, x_out, x_flush_sem)
-    x_flush.start()
-
-    def partial(t, q):
-        owner = lax.rem(z + 2 * nz - 1 - t, nz) if q < pair else lax.rem(z + 1 + t, nz)
+    def partial(t, k):
+        owner = lax.rem(z + nz + 1 + t, nz) if k % 2 else lax.rem(z + 2 * nz - 1 - t, nz)
         at = lax.rem(owner + nz + turn_of(m, nz), nz) * block
         return jnp.dot(
-            x[q].reshape(nz * rows, depth),
+            x[batches[k]].reshape(nz * rows, depth),
             w[:, pl.ds(pl.multiple_of(at, block), block)],
             preferred_element_type=jnp.float32,
         )
 
-    def pass_on(t, q, value):
-        sent[t, q] = value.astype(jnp.bfloat16)
-        to = lax.rem(z + 1, nz) if q < pair else lax.rem(z + nz - 1, nz)
-        send(sent.at[t, q], ring.at[t, q], ring_sent.at[t, q], ring_sem.at[t, q], (to, s, m))
-
-    def local_slope(q):
-        part = pl.ds(q * nz, nz)
+    def pass_on(t, k, value):
+        sent[t, k] = value.astype(jnp.bfloat16)
+        to = lax.rem(z + nz - 1, nz) if k % 2 else lax.rem(z + 1, nz)
+        send(sent.at[t, k], ring.at[t, k], ring_sent.at[t, k], ring_sem.at[t, k], (to, s, m))
+
+    for k in range(pair):
+        own_copy(k).wait()
+        for step in steps:
+            here = x.at[batches[k], lax.rem(z + nz - step, nz)]
+            await_bytes(here, x_sem.at[k, step])
+            send(here, here, y_sent.at[k, step], y_sem.at[k, step], partner)
+        pass_on(0, k, partial(0, k))
+    for k in range(pair, micro):
+        for step in range(nz):
+            await_bytes(x.at[batches[k], lax.rem(z + nz - step, nz)], y_sem.at[k - pair, step])
+        pass_on(0, k, partial(0, k))
+
+    def step_of(t, _):
+        @pl.when(t <= 2)
+        def _():
+            for half in range(pair):
+                q = (t - 1) * pair + half
+                x_t[:, pl.ds(pl.multiple_of(q * nz * rows, nz * rows), nz * rows)] = x[q].reshape(nz * rows, depth).T
+
+        for k in range(micro):
+            value = partial(t, k)
+            await_bytes(ring.at[t - 1, k], ring_sem.at[t - 1, k])
+            pass_on(t, k, value + ring[t - 1, k].astype(jnp.float32))
+        return 0
+
+    lax.fori_loop(1, nz - 1, step_of, 0)
+
+    def local_slope(part, q):
         return pltpu.make_async_copy(slope_in.at[part], slope.at[part], slope_sem.at[q])
 
-    order = [q // 2 + (q % 2) * pair for q in range(micro)]
-    for q in order:
-        pass_on(0, q, partial(0, q))
-
-    def step_of(t, _):
-        for q in order:
-            value = partial(t, q)
-            await_bytes(ring.at[t - 1, q], ring_sem.at[t - 1, q])
-            pass_on(t, q, value + ring[t - 1, q].astype(jnp.float32))
-        return 0
-
-    lax.fori_loop(1, nz - 1, step_of, 0)
-    for q in order:
-        value = partial(nz - 1, q)
-        await_bytes(ring.at[nz - 2, q], ring_sem.at[nz - 2, q])
-        value = gelu_slope(value + ring[nz - 2, q].astype(jnp.float32)).astype(jnp.bfloat16)
+    for k in range(micro):
+        value = partial(nz - 1, k)
+        await_bytes(ring.at[nz - 2, k], ring_sem.at[nz - 2, k])
+        value = gelu_slope(value + ring[nz - 2, k].astype(jnp.float32)).astype(jnp.bfloat16)
+        q = batches[k]
         part = pl.ds(q * nz, nz)
         slope_in[part] = value.reshape(nz, rows, block)
-        pl.when(at_home)(lambda: local_slope(q).start())
+        pl.when(at_home)(lambda: local_slope(part, q).start())
 
         @pl.when(jnp.logical_not(at_home))
         def _():
@@ -228,7 +236,6 @@
             value = value + jnp.where(m == part, carried[c].astype(jnp.float32), 0.0)
             product[c, part] = value.astype(jnp.bfloat16)
             send(product.at[c, part], inbox.at[c, m], out_sem.at[c], in_sem.at[c], (z, below, part))
-        pltpu.make_async_copy(h.at[c], hidden_out.at[c], flush_sem.at[c]).start()
 
     def advance(i, _):
         @pl.when(i < chunks)
@@ -250,6 +257,19 @@
             return 0
 
         lax.fori_loop(0, chunks, later, 0)
+
+    def mix_copy(k):
+        at = pl.ds(pl.multiple_of(k * block, block), block)
+        return pltpu.make_async_copy(mix.at[:, at], mix_out.at[:, at], mix_sem.at[k])
+
+    def mix_of(k, _):
+        at = pl.ds(pl.multiple_of(k * block, block), block)
+        value = jnp.dot(x_t[...], h[:, :, at].reshape(chunks * rows, block), preferred_element_type=jnp.float32)
+        mix[:, at] = ((chunks * rows) ** (-0.5) * value).astype(jnp.bfloat16)
+        mix_copy(k).start()
+        return 0
+
+    lax.fori_loop(0, nz, mix_of, 0)
 
     @pl.when(is_top)
     def _():
@@ -270,7 +290,6 @@
         def _():
             await_bytes(inbox.at[c], out_sem.at[c])
 
-        await_bytes(h.at[c], flush_sem.at[c])
         return 0
 
     lax.fori_loop(0, chunks, drain, 0)
@@ -280,11 +299,13 @@
         for q in range(micro):
             await_bytes(slope.at[pl.ds(0, nz)], slope_sent.at[q])
 
-    x_flush.wait()
-    for step in steps:
-        await_bytes(x.at[kept, z], x_sent.at[step])
-    for step in range(nz):
-        await_bytes(x.at[kept, z], y_sent.at[step])
+    for k in range(pair):
+        for step in steps:
+            await_bytes(x.at[0, 0], x_sent.at[k, step])
+        for step in range(nz):
+            await_bytes(x.at[0, 0], y_sent.at[k, step])
+    for k in range(nz):
+        mix_copy(k).wait()
 
     def drain_ring(t, _):
         for q in range(micro):
@@ -312,18 +333,18 @@
     return pl.pallas_call(
         layer_kernel,
         out_shape=(
-            jax.ShapeDtypeStruct((micro, nz, rows, depth), jnp.bfloat16),
-            jax.ShapeDtypeStruct((chunks, rows, columns), jnp.bfloat16),
+            jax.ShapeDtypeStruct((depth, columns), jnp.bfloat16),
             jax.ShapeDtypeStruct((micro, rows, columns), jnp.bfloat16),
         ),
         in_specs=[pl.BlockSpec(memory_space=pltpu.VMEM)] * 3,
         out_specs=(
             pl.BlockSpec(memory_space=pl.ANY),
-            pl.BlockSpec(memory_space=pl.ANY),
             pl.BlockSpec(memory_space=pltpu.VMEM),
         ),
         scratch_shapes=[
             buffer(micro, nz, rows, depth),
+            buffer(depth, chunks * rows),
+            buffer(depth, columns),
             buffer(nz - 1, micro, nz * rows, block),
             buffer(nz - 1, micro, nz * rows, block),
             buffer(columns, depth),
@@ -339,27 +360,26 @@
             dma((chunks, nz // 2)),
             dma((chunks,)),
             dma((chunks,)),
-            dma((chunks,)),
+            dma((nz,)),
             dma,
             dma,
             dma((micro,)),
             dma((micro,)),
             dma((micro,)),
             dma((micro,)),
-            dma((nz,)),
-            dma((nz,)),
-            dma((nz,)),
-            dma((nz,)),
-            dma,
+            dma((micro // 2, nz)),
+            dma((micro // 2, nz)),
+            dma((micro // 2, nz)),
+            dma((micro // 2, nz)),
+            dma((micro // 2,)),
             dma((nz - 1, micro)),
             dma((nz - 1, micro)),
-            dma,
         ],
         compiler_params=pltpu.CompilerParams(
             collective_id=cid, has_side_effects=True, vmem_limit_bytes=56 * 1024 * 1024
         ),
         cost_estimate=pl.CostEstimate(
-            flops=4 * chunks * rows * depth * columns,
+            flops=6 * chunks * rows * depth * columns,
             bytes_accessed=4 * depth * columns,
             transcendentals=0,
         ),
@@ -369,18 +389,13 @@
 def on_device(stash, w_mix, top_grad, order):
     micro = stash.shape[1]
     weight = w_mix[0]
-    depth, half = weight.shape
 
     series = jnp.arange(micro, dtype=jnp.int32)
     match = (order[0][None, :] == series[:, None]).astype(jnp.int32)
     slot_table = jnp.sum(series[None, :] * match, axis=1)
     x_own = jnp.take(stash[0], slot_table, axis=0)
-    x, hidden, input_grad = layers(x_own, weight, top_grad)
-    x = x.reshape(-1, depth)
-    grad_mix = x.shape[0] ** (-0.5) * lax.dot_general(
-        x, hidden.reshape(-1, half), (((0,), (0,)), ((), ())), preferred_element_type=jnp.float32
-    )
-    return (input_grad[None], grad_mix.astype(jnp.bfloat16)[None])
+    grad_mix, input_grad = layers(x_own, weight, top_grad)
+    return (input_grad[None], grad_mix[None])
 
 
 def solution(mesh):

time: 483 us -> 473 us (0.979)
  matrix products: 9.15 us -> 0 us
  Pallas kernels: 468 us -> 461 us
  local copies, waits for them, and re-layouts: 2.94 us -> 8.96 us
    dot_general x1 -> x0, matrix products: 9.15 us -> none  [on_device(): lax.dot_general(x, hidden.reshape(-1, half), (((0,), (0,)), ((), ())), pr...]
    pallas_call x1, Pallas kernels: 468 us -> 461 us  [layers(): pl.pallas_call(layer_kernel, out_shape=(jax.ShapeDtypeStruct((depth, colu...]
    unnamed x5 -> x4, local copies, waits for them, and re-layouts: 2.29 us -> 8.31 us
where the time goes in v4:
time: 473 us
  Pallas kernels  461 us (97%)
  local copies, waits for them, and re-layouts  8.96 us (2%)
    pallas_call x1, Pallas kernels, layers(): pl.pallas_call(layer_kernel, out_shape=(jax.ShapeDtypeStruct((depth, colu...  461 us

profile of v4, /device:TPU:1, one launch (start us, length us, event | category | flops | bytes accessed | tf_op | source)
XLA Modules:
  0.0 473.2 jit_solution(6610052528190610700)
XLA Ops:
  0.6 0.0 copy-start
  0.6 1.4 copy-done
  2.0 0.8 select_reduce_fusion
  2.8 0.6 gather_fusion
  3.5 1.4 broadcast_select_fusion.x_own
  4.9 461.4 %shard_map.59 = (bf16[768,3072]{1,0:T(8,128)(2,1)}, bf16[4,32,3072]{2,1,0:T(8,128)(2,1)}) custom-call(bf16[4,32,6144]{2,1,0:T(8,128)(2,1)} %broadcast_select_fusion.x_own, bf16[768,3072]{1,0:T(8,128)(2,1)} %bitcast.12, bf16[4,32,3072]{2,1,0:T(8,128)(2,1)} %top.1), custom_call_target="tpu_custom_call" | custom-call | flops 14495514624 | bytes 9437184 | tf_op jit(solution)/shard_map/pallas_call | solution.py:333
  466.3 2.1 copy.8
  468.3 4.8 %copy.9 = bf16[1,768,3072]{2,1,0:T(8,128)(2,1)} copy(bf16[1,768,3072]{2,1,0:T(8,128)(2,1)} %bitcast.10) | data formatting | bytes 9437184
  (3 shorter events, 0.0 us)
Async XLA Ops:
  0.6 1.4 copy-start

commit v5 on v4

--- a/solution.py
+++ b/solution.py
@@ -6,7 +6,8 @@
 from jax.sharding import PartitionSpec as P
 
 MESH = pl.DeviceIdType.MESH
-LAG = 1
+LAG = 2
+ROWS = 16
 
 
 def gelu_slope(value):
@@ -35,9 +36,10 @@
     nz, ns = lax.axis_size("dp"), lax.axis_size("section")
     z, s, m = lax.axis_index("dp"), lax.axis_index("section"), lax.axis_index("mp")
     chunks, rows, columns = h.shape
-    micro = chunks // nz
+    micro, _, whole, depth = x.shape
+    per = whole // rows
+    share_of = nz * per
     block = columns // nz
-    depth = x.shape[-1]
     pair = micro // 2
     steps = sorted(range(1, nz), key=lambda k: min(k, nz - k))
     partner = (z, s, 1 - m)
@@ -101,14 +103,15 @@
         def spread(q, _):
             def give(step):
                 to = lax.rem(own + step, nz)
-                send(top.at[q, :, place(to)], carried.at[q * nz + z], top_sent.at[q], top_sem.at[q], owner_of(to))
+                src, dst = top.at[pl.ds(q * per, per), :, place(to)], carried.at[pl.ds((q * nz + z) * per, per)]
+                send(src, dst, top_sent.at[q], top_sem.at[q], owner_of(to))
 
             for step in range(nz):
                 each_other(step, give)
 
             @pl.when(in_column)
             def _():
-                carried[q * nz + z] = top[q, :, mine]
+                carried[pl.ds((q * nz + z) * per, per)] = top[pl.ds(q * per, per), :, mine]
 
             return 0
 
@@ -125,7 +128,7 @@
         owner = lax.rem(z + nz + 1 + t, nz) if k % 2 else lax.rem(z + 2 * nz - 1 - t, nz)
         at = lax.rem(owner + nz + turn_of(m, nz), nz) * block
         return jnp.dot(
-            x[batches[k]].reshape(nz * rows, depth),
+            x[batches[k]].reshape(nz * whole, depth),
             w[:, pl.ds(pl.multiple_of(at, block), block)],
             preferred_element_type=jnp.float32,
         )
@@ -152,7 +155,7 @@
         def _():
             for half in range(pair):
                 q = (t - 1) * pair + half
-                x_t[:, pl.ds(pl.multiple_of(q * nz * rows, nz * rows), nz * rows)] = x[q].reshape(nz * rows, depth).T
+                x_t[:, pl.ds(pl.multiple_of(q * nz * whole, nz * whole), nz * whole)] = x[q].reshape(nz * whole, depth).T
 
         for k in range(micro):
             value = partial(t, k)
@@ -170,34 +173,34 @@
         await_bytes(ring.at[nz - 2, k], ring_sem.at[nz - 2, k])
         value = gelu_slope(value + ring[nz - 2, k].astype(jnp.float32)).astype(jnp.bfloat16)
         q = batches[k]
-        part = pl.ds(q * nz, nz)
-        slope_in[part] = value.reshape(nz, rows, block)
+        part = pl.ds(q * share_of, share_of)
+        slope_in[part] = value.reshape(share_of, rows, block)
         pl.when(at_home)(lambda: local_slope(part, q).start())
 
         @pl.when(jnp.logical_not(at_home))
         def _():
             send(slope_in.at[part], slope.at[part], slope_sent.at[q], slope_sem.at[q], owner_of(number))
 
-    def await_blocks(ref, sem):
-        pl.when(in_column)(lambda: await_bytes(ref.at[pl.ds(0, nz - 1)], sem))
-        pl.when(jnp.logical_not(in_column))(lambda: await_bytes(ref.at[pl.ds(0, nz)], sem))
+    def await_blocks(ref, sem, size=1):
+        pl.when(in_column)(lambda: await_bytes(ref.at[pl.ds(0, (nz - 1) * size)], sem))
+        pl.when(jnp.logical_not(in_column))(lambda: await_bytes(ref.at[pl.ds(0, nz * size)], sem))
 
     def received(c):
         await_bytes(inbox.at[c], in_sem.at[c])
         return (inbox[c, 0].astype(jnp.float32) + inbox[c, 1].astype(jnp.float32)).astype(jnp.bfloat16)
 
     def send_back(c):
-        q, d = c // nz, lax.rem(c, nz)
-        send(carried.at[c], back.at[q, :, mine], back_sent, back_sem, (d, above, to_m))
+        at = c // share_of * per + lax.rem(c, per)
+        send(carried.at[c], back.at[at, :, mine], back_sent, back_sem, (lax.rem(c // per, nz), above, to_m))
 
     def publish(c):
-        @pl.when(lax.rem(c, nz) == 0)
-        def _():
-            await_bytes(slope.at[pl.ds(c, nz)], slope_sem.at[c // nz])
+        @pl.when(lax.rem(c, share_of) == 0)
+        def _():
+            await_bytes(slope.at[pl.ds(c, share_of)], slope_sem.at[c // share_of])
 
             @pl.when(is_top)
             def _():
-                await_blocks(carried, top_sem.at[c // nz])
+                await_blocks(carried, top_sem.at[c // share_of], per)
 
         @pl.when(jnp.logical_not(is_top))
         def _():
@@ -207,7 +210,7 @@
         shared[c] = value
 
         def share(step):
-            send(shared.at[c], h.at[c, :, mine], copy_sem.at[c], h_sem.at[c, own // 2], (lax.rem(z + step, nz), s, to_m))
+            send(shared.at[c], h.at[c, :, mine], copy_sem.at[c], h_sem.at[c], (lax.rem(z + step, nz), s, to_m))
 
         for step in sorted(range(nz), key=lambda k: -min(k, nz - k)):
             each_other(step, share)
@@ -216,21 +219,9 @@
         def _():
             h[c, :, mine] = value
 
-    sources = nz // 2
-    nearest = jnp.where(in_column, z, z + 1)
-
     def multiply(c):
-        total = None
-        for k in range(sources):
-            near = lax.rem(nearest + k, sources)
-            if k:
-                await_bytes(shared.at[pl.ds(0, 2)], h_sem.at[c, near])
-            else:
-                pl.when(in_column)(lambda: await_bytes(shared.at[0], h_sem.at[c, near]))
-                pl.when(jnp.logical_not(in_column))(lambda: await_bytes(shared.at[pl.ds(0, 2)], h_sem.at[c, near]))
-            at = pl.ds(pl.multiple_of(near * 2 * block, 2 * block), 2 * block)
-            term = jnp.dot(h[c, :, at], w_t[at, :], preferred_element_type=jnp.float32)
-            total = term if total is None else total + term
+        await_blocks(shared, h_sem.at[c])
+        total = jnp.dot(h[c], w_t[...], preferred_element_type=jnp.float32)
         for part in range(2):
             value = total[:, part * block : (part + 1) * block]
             value = value + jnp.where(m == part, carried[c].astype(jnp.float32), 0.0)
@@ -281,7 +272,7 @@
 
         lax.fori_loop(0, chunks, last, 0)
         for q in range(micro):
-            await_blocks(shared, top_sent.at[q])
+            await_blocks(shared, top_sent.at[q], per)
 
     def drain(c, _):
         await_blocks(shared, copy_sem.at[c])
@@ -297,7 +288,7 @@
     @pl.when(jnp.logical_not(at_home))
     def _():
         for q in range(micro):
-            await_bytes(slope.at[pl.ds(0, nz)], slope_sent.at[q])
+            await_bytes(slope.at[pl.ds(0, share_of)], slope_sent.at[q])
 
     for k in range(pair):
         for step in steps:
@@ -321,20 +312,22 @@
 
 def layers(x_own, w, top, cid=0):
     nz = lax.axis_size("dp")
-    micro, rows, _ = x_own.shape
+    micro, whole, _ = x_own.shape
+    rows = min(ROWS, whole)
+    per = whole // rows
     depth, columns = w.shape
     block = columns // nz
-    chunks = micro * nz
+    chunks = micro * nz * per
     dma = pltpu.SemaphoreType.DMA
 
     def buffer(*shape):
         return pltpu.VMEM(shape, jnp.bfloat16)
 
-    return pl.pallas_call(
+    mix, back = pl.pallas_call(
         layer_kernel,
         out_shape=(
             jax.ShapeDtypeStruct((depth, columns), jnp.bfloat16),
-            jax.ShapeDtypeStruct((micro, rows, columns), jnp.bfloat16),
+            jax.ShapeDtypeStruct((micro * per, rows, columns), jnp.bfloat16),
         ),
         in_specs=[pl.BlockSpec(memory_space=pltpu.VMEM)] * 3,
         out_specs=(
@@ -342,11 +335,11 @@
             pl.BlockSpec(memory_space=pltpu.VMEM),
         ),
         scratch_shapes=[
-            buffer(micro, nz, rows, depth),
+            buffer(micro, nz, whole, depth),
             buffer(depth, chunks * rows),
             buffer(depth, columns),
-            buffer(nz - 1, micro, nz * rows, block),
-            buffer(nz - 1, micro, nz * rows, block),
+            buffer(nz - 1, micro, nz * whole, block),
+            buffer(nz - 1, micro, nz * whole, block),
             buffer(columns, depth),
             buffer(chunks, rows, block),
             buffer(chunks, rows, columns),
@@ -355,9 +348,9 @@
             buffer(chunks, rows, block),
             buffer(chunks, 2, rows, block),
             buffer(chunks, rows, block),
-            buffer(micro, rows, columns),
+            buffer(micro * per, rows, columns),
             dma((chunks,)),
-            dma((chunks, nz // 2)),
+            dma((chunks,)),
             dma((chunks,)),
             dma((chunks,)),
             dma((nz,)),
@@ -383,7 +376,8 @@
             bytes_accessed=4 * depth * columns,
             transcendentals=0,
         ),
-    )(x_own, w, top)
+    )(x_own, w, top.reshape(micro * per, rows, columns))
+    return mix, back.reshape(micro, whole, columns)
 
 
 def on_device(stash, w_mix, top_grad, order):

time: 473 us -> 450 us (0.951)
  Pallas kernels: 461 us -> 438 us
    pallas_call x1, Pallas kernels: 461 us -> 438 us  [layers(): pl.pallas_call(layer_kernel, out_shape=(jax.ShapeDtypeStruct((depth, colu...]
where the time goes in v5:
time: 450 us
  Pallas kernels  438 us (97%)
  local copies, waits for them, and re-layouts  8.96 us (2%)
    pallas_call x1, Pallas kernels, layers(): pl.pallas_call(layer_kernel, out_shape=(jax.ShapeDtypeStruct((depth, colu...  438 us

profile of v5, /device:TPU:1, one launch (start us, length us, event | category | flops | bytes accessed | tf_op | source)
XLA Modules:
  0.0 450.0 jit_solution(15883371665922038257)
XLA Ops:
  0.6 0.0 copy-start
  0.6 1.4 copy-done
  2.0 0.8 select_reduce_fusion
  2.8 0.6 gather_fusion
  3.5 1.4 broadcast_select_fusion.x_own
  4.9 438.2 %shard_map.59 = (bf16[768,3072]{1,0:T(8,128)(2,1)}, bf16[8,16,3072]{2,1,0:T(8,128)(2,1)}) custom-call(bf16[4,32,6144]{2,1,0:T(8,128)(2,1)} %broadcast_select_fusion.x_own, bf16[768,3072]{1,0:T(8,128)(2,1)} %bitcast.13, bf16[8,16,3072]{2,1,0:T(8,128)(2,1)} %bitcast.14), custom_call_target="tpu_custom_call" | custom-call | flops 14495514624 | bytes 9437184 | tf_op jit(solution)/shard_map/pallas_call | solution.py:326
  443.1 2.1 copy.8
  445.2 4.8 %copy.9 = bf16[1,768,3072]{2,1,0:T(8,128)(2,1)} copy(bf16[1,768,3072]{2,1,0:T(8,128)(2,1)} %bitcast.11) | data formatting | bytes 9437184
  (3 shorter events, 0.0 us)
Async XLA Ops:
  0.6 1.4 copy-start

commit v6 on v5

--- a/solution.py
+++ b/solution.py
@@ -228,6 +228,26 @@
             product[c, part] = value.astype(jnp.bfloat16)
             send(product.at[c, part], inbox.at[c, m], out_sem.at[c], in_sem.at[c], (z, below, part))
 
+    def settle():
+        @pl.when(jnp.logical_not(at_home))
+        def _():
+            for q in range(micro):
+                await_bytes(slope.at[pl.ds(0, share_of)], slope_sent.at[q])
+
+        for k in range(pair):
+            for step in steps:
+                await_bytes(x.at[0, 0], x_sent.at[k, step])
+            for step in range(nz):
+                await_bytes(x.at[0, 0], y_sent.at[k, step])
+        def drain_ring(t, _):
+            for q in range(micro):
+                await_bytes(sent.at[t, q], ring_sent.at[t, q])
+            return 0
+
+        lax.fori_loop(0, nz - 1, drain_ring, 0)
+
+    pl.when(jnp.logical_not(is_top))(settle)
+
     def advance(i, _):
         @pl.when(i < chunks)
         def _():
@@ -243,11 +263,12 @@
 
     @pl.when(jnp.logical_not(is_top))
     def _():
-        def later(c, _):
-            send_back(c)
+        def later(j, _):
+            src, dst = carried.at[pl.ds(j * per, per)], back.at[pl.ds(j // nz * per, per), :, mine]
+            send(src, dst, back_sent, back_sem, (lax.rem(j, nz), above, to_m))
             return 0
 
-        lax.fori_loop(0, chunks, later, 0)
+        lax.fori_loop(0, chunks // per, later, 0)
 
     def mix_copy(k):
         at = pl.ds(pl.multiple_of(k * block, block), block)
@@ -285,25 +306,9 @@
 
     lax.fori_loop(0, chunks, drain, 0)
 
-    @pl.when(jnp.logical_not(at_home))
-    def _():
-        for q in range(micro):
-            await_bytes(slope.at[pl.ds(0, share_of)], slope_sent.at[q])
-
-    for k in range(pair):
-        for step in steps:
-            await_bytes(x.at[0, 0], x_sent.at[k, step])
-        for step in range(nz):
-            await_bytes(x.at[0, 0], y_sent.at[k, step])
+    pl.when(is_top)(settle)
     for k in range(nz):
         mix_copy(k).wait()
-
-    def drain_ring(t, _):
-        for q in range(micro):
-            await_bytes(sent.at[t, q], ring_sent.at[t, q])
-        return 0
-
-    lax.fori_loop(0, nz - 1, drain_ring, 0)
 
     await_bytes(back, back_sem)
     grad_out[...] = back[...]

time: 450 us -> 451 us (level)
  no operation moved by 1% of the time
where the time goes in v6:
time: 451 us; the launch traced here: 450 us
  Pallas kernels  439 us (97%)
  local copies, waits for them, and re-layouts  8.96 us (2%)
    pallas_call x1, Pallas kernels, layers(): pl.pallas_call(layer_kernel, out_shape=(jax.ShapeDtypeStruct((depth, colu...  439 us

profile of v6, /device:TPU:1, one launch (start us, length us, event | category | flops | bytes accessed | tf_op | source)
XLA Modules:
  0.0 450.4 jit_solution(15994650712379184433)
XLA Ops:
  0.6 0.0 copy-start
  0.6 1.4 copy-done
  2.0 0.8 select_reduce_fusion
  2.8 0.6 gather_fusion
  3.5 1.4 broadcast_select_fusion.x_own
  4.9 438.6 %shard_map.59 = (bf16[768,3072]{1,0:T(8,128)(2,1)}, bf16[8,16,3072]{2,1,0:T(8,128)(2,1)}) custom-call(bf16[4,32,6144]{2,1,0:T(8,128)(2,1)} %broadcast_select_fusion.x_own, bf16[768,3072]{1,0:T(8,128)(2,1)} %bitcast.13, bf16[8,16,3072]{2,1,0:T(8,128)(2,1)} %bitcast.14), custom_call_target="tpu_custom_call" | custom-call | flops 14495514624 | bytes 9437184 | tf_op jit(solution)/shard_map/pallas_call | solution.py:331
  443.5 2.1 copy.8
  445.6 4.8 %copy.9 = bf16[1,768,3072]{2,1,0:T(8,128)(2,1)} copy(bf16[1,768,3072]{2,1,0:T(8,128)(2,1)} %bitcast.11) | data formatting | bytes 9437184
  (3 shorter events, 0.0 us)
Async XLA Ops:
  0.6 1.4 copy-start
